TPU v7x, 256 devices: a whole 4x4x8 slice. The times are simulated.
256 devices in a mesh: inst: 32 (over z, x), tp: 8 (over y, core).
Axes of the slice: x: 4, y: 4, z: 8, core: 2. Of those that a mesh axis runs over, the one named last changes fastest.
Arguments:
- hidden: bfloat16 [64, 8192], P(None, 'inst'), may hold values from -400 to 400
- norm_gain: bfloat16 [8192], P('inst'), may hold values from 0.099609375 to 1.8984375
- w_query: bfloat16 [8192, 8192], P('inst', 'tp'), may hold values from -0.0625 to 0.0625
- w_key: bfloat16 [8192, 1024], P('inst', 'tp'), may hold values from -0.15625 to 0.15625
- w_value: bfloat16 [8192, 1024], P('inst', 'tp'), may hold values from -0.0625 to 0.0625
- w_out: bfloat16 [8192, 8192], P('tp', 'inst'), may hold values from -0.0625 to 0.0625
- kv_cache: bfloat16 [2, 1024, 256, 1024], P(None, 'inst', None, 'tp'), may hold values from -256 to 256
- lengths: int32 [32], replicated, may hold values from 1 to 8192, as said below
- slot_owner: int32 [1024], P('inst'), may hold values from -1 to 31, as said below
- slot_page: int32 [1024], P('inst'), may hold values from 0 to 31, as said below
Outputs:
- mixed: bfloat16 [64, 8192], P(None, 'inst')
Inputs may be any that keep to these rules, and one draw needn't show every extreme that they name: `lengths`: A request holds ceil(length / 256) page slots; exactly one request has 32 full pages (length 8192). `slot_owner`: every request owns one or more slots; on each index of inst the live slots come first, and on some index all 32 slots are live and belong to one request. `slot_page`: the slots of one request hold its pages 0, 1, ... without gaps or repeats; empty slots hold 0.
All inputs are finite; a program needn't handle non-finite values.
Results may differ from a plain program's by a relative error of at most 0.0093.
Values may be sent and summed in bfloat16 or wider, within the bound.
A program may use at most 64 MiB of HBM per device.

v0:
```python
import jax
import jax.numpy as jnp
from jax import lax
from jax.sharding import PartitionSpec as P

D = 8192
HD = 128


NEG = -1e30
EPS = 1e-05
THETA = 500000.0


def joined_2(x, axis, combine):
    everything = jax.tree.map(lambda part: lax.all_gather(part, axis), x)
    first = jax.tree.map(lambda part: part[0], everything)

    def lap(k, so_far):
        return combine(so_far, jax.tree.map(lambda part: part[k], everything))

    return lax.fori_loop(1, lax.axis_size(axis), lap, first)


def rotate(vector, positions, head_count):
    head_width = vector.shape[-1] // head_count
    halfway = head_width // 2
    inverse = THETA ** (-(jnp.arange(halfway, dtype=jnp.float32) * (2.0 / head_width)))
    angles = positions.astype(jnp.float32)[:, None] * inverse[None, :]
    cosine = jnp.cos(angles)[:, None, :]
    sine_part = jnp.sin(angles)[:, None, :]
    per_head = vector.reshape(vector.shape[0], head_count, head_width)
    first_half = per_head[..., :halfway]
    second_half = per_head[..., halfway:]
    turned = jnp.concatenate(
        [
            first_half * cosine - second_half * sine_part,
            second_half * cosine + first_half * sine_part,
        ],
        axis=-1,
    )
    return turned.reshape(vector.shape)


def soft_terms(scores, keep_mask, values_block, out_form):
    scores = jnp.where(keep_mask, scores, NEG)
    top_score = jnp.max(scores, axis=-1)
    weights = jnp.where(keep_mask, jnp.exp(scores - top_score[..., None]), 0.0)
    weight_sum = jnp.sum(weights, axis=-1)
    output = jnp.einsum(
        out_form, weights.astype(jnp.bfloat16), values_block, preferred_element_type=jnp.float32
    )
    return (top_score, weight_sum, output)


def slot_terms(queries, lengths, owners, page_ids, cache_block):
    slot_count = owners.shape[0]
    page_len = cache_block.shape[2]
    local_kv = queries.shape[2]
    head_dim = queries.shape[-1]
    owner_safe = jnp.maximum(owners, 0)
    query_rows = queries[owner_safe]
    offsets = page_ids[:, None] * page_len + jnp.arange(page_len, dtype=jnp.int32)[None, :]
    valid_mask = (owners[:, None] >= 0) & (offsets < lengths[owner_safe][:, None])
    keys_block = cache_block[0].reshape(slot_count, page_len, local_kv, head_dim)
    values_block = cache_block[1].reshape(slot_count, page_len, local_kv, head_dim)
    scores = jnp.einsum(
        "stkgd,spkd->stkgp", query_rows, keys_block, preferred_element_type=jnp.float32
    ) * head_dim ** (-0.5)
    return soft_terms(scores, valid_mask[:, None, None, None, :], values_block, "stkgp,spkd->stkgd")


def fresh_terms(queries, keys_new, values_new):
    new_count = queries.shape[1]
    head_dim = queries.shape[-1]
    scores = jnp.einsum(
        "ntkgd,nukd->ntkgu", queries, keys_new, preferred_element_type=jnp.float32
    ) * head_dim ** (-0.5)
    causal = jnp.arange(new_count)[None, :] <= jnp.arange(new_count)[:, None]
    return soft_terms(scores, causal[None, :, None, None, :], values_new, "ntkgu,nukd->ntkgd")


def join(first_part, second_part):
    peak_score = jnp.maximum(first_part[0], second_part[0])
    scale_first = jnp.exp(first_part[0] - peak_score)
    scale_second = jnp.exp(second_part[0] - peak_score)
    return (
        peak_score,
        scale_first * first_part[1] + scale_second * second_part[1],
        scale_first[..., None] * first_part[2] + scale_second[..., None] * second_part[2],
    )


def finish_attention(combined, queries, keys_new, values_new):
    request_count = queries.shape[0]
    fresh_top, fresh_sum, fresh_out = fresh_terms(queries, keys_new, values_new)
    fresh_block = (
        fresh_top.reshape(request_count, -1),
        fresh_sum.reshape(request_count, -1),
        fresh_out.reshape(request_count, -1, fresh_out.shape[-1]),
    )
    joined = join(combined, fresh_block)
    attention = joined[2] / joined[1][..., None]
    return attention.astype(jnp.bfloat16).reshape(request_count * queries.shape[1], -1)


def on_device(
    hidden, norm_gain, w_query, w_key, w_value, w_out, kv_cache, lengths, slot_owner, slot_page
):
    tokens = hidden.shape[0]
    requests = lengths.shape[0]
    new_count = tokens // requests
    local_q = w_query.shape[1] // HD
    local_kv = w_key.shape[1] // HD
    group_size = local_q // local_kv
    query_cols = local_q * HD
    kv_cols = local_kv * HD
    floats = hidden.astype(jnp.float32)
    local_squares = jnp.sum(floats * floats, axis=1)
    normed = (floats * norm_gain.astype(jnp.float32)[None, :]).astype(jnp.bfloat16)
    positions = (lengths[:, None] + jnp.arange(new_count, dtype=jnp.int32)[None, :]).reshape(-1)
    joined, squares = lax.psum(
        (
            jnp.concatenate(
                [
                    jnp.dot(normed, w_query, preferred_element_type=jnp.float32),
                    jnp.dot(normed, w_key, preferred_element_type=jnp.float32),
                    jnp.dot(normed, w_value, preferred_element_type=jnp.float32),
                ],
                axis=1,
            ),
            local_squares,
        ),
        "inst",
    )
    inverse = lax.rsqrt(squares / D + EPS)
    finish_joined = joined * inverse[:, None]
    query_part = rotate(finish_joined[:, :query_cols], positions, local_q).astype(jnp.bfloat16)
    key_part = rotate(
        finish_joined[:, query_cols : query_cols + kv_cols], positions, local_kv
    ).astype(jnp.bfloat16)
    value_part = finish_joined[:, query_cols + kv_cols :].astype(jnp.bfloat16)
    queries = query_part
    keys_new = key_part
    values_new = value_part
    queries = queries.reshape(requests, new_count, local_kv, group_size, HD)
    keys_new = keys_new.reshape(requests, new_count, local_kv, HD)
    values_new = values_new.reshape(requests, new_count, local_kv, HD)
    slots = slot_owner.shape[0]
    top_slot, sum_slot, out_slot = slot_terms(queries, lengths, slot_owner, slot_page, kv_cache)
    flat_width = new_count * local_q
    top_slot = top_slot.reshape(slots, flat_width)
    sum_slot = sum_slot.reshape(slots, flat_width)
    out_slot = out_slot.reshape(slots, flat_width, HD)
    member = slot_owner[:, None] == jnp.arange(requests, dtype=jnp.int32)[None, :]
    top_owner = jnp.max(jnp.where(member[:, :, None], top_slot[:, None, :], NEG), axis=0)
    factor = jnp.exp(top_slot - top_owner[jnp.maximum(slot_owner, 0)])
    onehot = member.astype(jnp.float32)
    sum_owner = jnp.einsum("sr,sq->rq", onehot, factor * sum_slot, precision=lax.Precision.HIGHEST)
    out_owner = jnp.einsum(
        "sr,sqd->rqd", onehot, factor[..., None] * out_slot, precision=lax.Precision.HIGHEST
    )
    merged = joined_2((top_owner, sum_owner, out_owner), "inst", join)
    attention = finish_attention(merged, queries, keys_new, values_new)
    partial_value = jnp.dot(attention, w_out, preferred_element_type=jnp.float32)
    return lax.psum(partial_value, "tp").astype(jnp.bfloat16)


def solution(mesh):
    return jax.shard_map(
        on_device,
        mesh=mesh,
        in_specs=(
            P(None, "inst"),
            P("inst"),
            P("inst", "tp"),
            P("inst", "tp"),
            P("inst", "tp"),
            P("tp", "inst"),
            P(None, "inst", None, "tp"),
            P(),
            P("inst"),
            P("inst"),
        ),
        out_specs=P(None, "inst"),
        check_vma=False,
    )
```

profile of v0, /device:TPU:1, one launch (start us, length us, event | category | flops | bytes accessed | tf_op | source)
XLA Modules:
  0.0 343.8 jit_solution(11208592192871740345)
XLA Ops:
  7.3 1.0 fusion.55
  8.2 1.0 fusion.53
  14.6 64.4 %psum.22 = f32[64]{0:T(128)S(1)} all-reduce(f32[64]{0:T(128)S(1)} %fusion.41), channel_id=1, replica_groups=mesh['inst'=32,'tp'=8] {'inst'}, use_global_device_ids=true, to_apply=%region_2.0 | all-reduce | flops 64 | bytes 512 | tf_op jit(solution)/shard_map/psum | solution.py:122
  79.7 1.4 gather_fusion
  81.6 73.6 %all-reduce.2.cloned.1.call-done = f32[64,1280]{1,0:T(8,128)} async-done(((f32[64,1280]{1,0:T(8,128)}), f32[64,1280]{1,0:T(8,128)}) %all-reduce.2.cloned.1.call-update) | async-done | bytes 327696 | tf_op jit(solution)/shard_map/psum | solution.py:122
  155.2 1.1 broadcast_multiply_fusion
  157.2 2.3 fusion.71
  160.6 2.0 fusion.22
  162.7 1.1 fusion.35
  165.7 38.0 %all-gather.4 = f32[32,32,16]{1,2,0:T(8,128)S(1)} all-gather(f32[1,32,16]{1,2,0:T(8,128)S(1)} %convolution_bitcast_fusion.1), channel_id=3, replica_groups=mesh['inst'=32,'tp'=8] {'inst'}, dimensions={0}, use_global_device_ids=true | all-gather | bytes 67584 | tf_op jit(solution)/shard_map/all_gather | solution.py:16
  203.7 37.4 %all-gather.3 = f32[32,32,16]{1,2,0:T(8,128)S(1)} all-gather(f32[1,32,16]{1,2,0:T(8,128)S(1)} %bitcast.143), channel_id=2, replica_groups=mesh['inst'=32,'tp'=8] {'inst'}, dimensions={0}, use_global_device_ids=true | all-gather | bytes 67584 | tf_op jit(solution)/shard_map/all_gather | solution.py:16
  241.1 24.2 %all-gather.7.cloned.1.call-done = f32[1024,16,128]{2,0,1:T(8,128)} async-done(((f32[32,16,128]{2,0,1:T(8,128)}), f32[1024,16,128]{2,0,1:T(8,128)}) %all-gather.7.cloned.1.call-update) | async-done | bytes 8388624 | tf_op jit(solution)/shard_map/all_gather | solution.py:16
  266.4 45.8 %while.19 = (s32[]{:T(128)}, f32[32,16]{0,1:T(8,128)S(1)}, f32[32,16]{0,1:T(8,128)S(1)}, f32[32,16,128]{2,1,0:T(8,128)S(1)}, f32[32,32,16]{1,2,0:T(8,128)S(1)}, ...) while((s32[]{:T(128)}, f32[32,16]{0,1:T(8,128)S(1)}, ...), condition=%wide.region_7.8_spmd, body=%wide.region_6.7_spmd.sunk | while | flops 199685 | bytes 1339535 | solution.py:22
  266.6 1.0 constant_dynamic-slice_fusion.2
  269.6 1.0 constant_dynamic-slice_fusion.2
  271.1 1.0 constant_dynamic-slice_fusion.2
  272.5 1.0 constant_dynamic-slice_fusion.2
  274.0 1.0 constant_dynamic-slice_fusion.2
  275.5 1.0 constant_dynamic-slice_fusion.2
  277.0 1.0 constant_dynamic-slice_fusion.2
  278.4 1.0 constant_dynamic-slice_fusion.2
  279.9 1.0 constant_dynamic-slice_fusion.2
  281.4 1.0 constant_dynamic-slice_fusion.2
  313.2 23.8 %psum.23 = bf16[64,256]{1,0:T(8,128)(2,1)} all-reduce(f32[64,256]{1,0:T(8,128)S(1)} %fusion.73), channel_id=1, replica_groups=mesh['inst'=32,'tp'=8] {'tp'}, use_global_device_ids=true, to_apply=%region_10.11 | all-reduce | flops 16384 | bytes 98304 | tf_op jit(solution)/shard_map/psum | solution.py:166
  (206 shorter events, 48.1 us)
Async XLA Ops:
  6.5 2.7 copy-start
  6.5 148.7 %all-reduce.2.cloned.1.call-start = ((), (), s32[]{:S(2)}) async-start(), calls=%async_computation | async-start | bytes 655360 | tf_op jit(solution)/shard_map/psum | solution.py:122
  11.0 254.3 %all-gather.7.cloned.1.call-start = ((), (), s32[]{:S(2)}) async-start(), calls=%async_computation.1 | async-start | bytes 8650752 | tf_op jit(solution)/shard_map/all_gather | solution.py:16
  156.3 6.4 %copy-start.2 = (s32[32]{0:T(128)S(1)}, s32[32]{0:T(128)}, u32[]{:S(2)}) copy-start(s32[32]{0:T(128)} %param.20) | copy-start | bytes 388
  266.4 46.6 %copy-start.1 = (bf16[1024,256]{1,0:T(8,128)(2,1)S(1)}, bf16[1024,256]{1,0:T(8,128)(2,1)}, u32[]{:S(2)}) copy-start(bf16[1024,256]{1,0:T(8,128)(2,1)} %param.17) | copy-start | bytes 1572868
Sparse Core Ops, SparseCore 0:
  11.1 144.0 all-reduce.1
  163.9 101.3 all-gather.6
where the time goes:
time: 346 us; the launch traced here: 344 us
  blocking collectives  164 us (47%)
  waiting for transfers between devices  97.8 us (28%)
  local copies, waits for them, and re-layouts  39.5 us (11%)
  other arithmetic  18.2 us (5%)
  between operations  13.6 us (4%)
  matrix products  9.9 us (3%)
    all_gather x2, blocking collectives, joined_2(): everything = jax.tree.map(lambda part: lax.all_gather(part, axis), x)  75.4 us
    psum x1, waiting for transfers between devices, on_device(): lax.psum((jnp.concatenate([jnp.dot(normed, w_query, preferred_element_typ...  73.6 us
    psum x1, blocking collectives, on_device(): lax.psum((jnp.concatenate([jnp.dot(normed, w_query, preferred_element_typ...  64.4 us
    dynamic_slice x31, local copies, waits for them, and re-layouts, lap(): return combine(so_far, jax.tree.map(lambda part: part[k], everything))  30.2 us
    all_gather x1, waiting for transfers between devices, joined_2(): everything = jax.tree.map(lambda part: lax.all_gather(part, axis), x)  24.2 us
    psum x1, blocking collectives, on_device(): return lax.psum(partial_value, 'tp').astype(jnp.bfloat16)  23.8 us
    add x31, other arithmetic, join(): scale_first[..., None] * first_part[2]  9.35 us
  transfers between devices with their start and end apart: 2, of which 2 were waited for; matrix products, arithmetic and copies ran while one was open for 2% of the time, Pallas kernels for 0%

commit v1 on v0

v1 whole, which is shorter than its diff:
```python
import functools

import jax
import jax.numpy as jnp
from jax import lax
from jax.experimental import pallas as pl
from jax.experimental.pallas import tpu as pltpu
from jax.sharding import PartitionSpec as P

D = 8192
HD = 128
NEG = -1e30
EPS = 1e-05
THETA = 500000.0
SCALE = HD ** -0.5
N_INST = 32
N_TP = 8
OWNERS = 16
MESH = pl.DeviceIdType.MESH
F32 = jnp.float32
BF16 = jnp.bfloat16


def iota(shape, dim):
    return lax.broadcasted_iota(jnp.int32, shape, dim)


def far_first(k):
    kz, kx = k // 4, k % 4
    dz = lax.rem(4 + (1 - 2 * lax.rem(kz, 2)) * ((kz + 1) // 2), 8)
    dx = lax.rem(2 + (1 - 2 * lax.rem(kx, 2)) * ((kx + 1) // 2), 4)
    return dz, dx


def rope(rows, cosine, sine):
    return rows * cosine + pltpu.roll(rows, 64, 1) * sine


def kernel(
    hid_hbm, gain_ref, wq_hbm, wk_hbm, wv_hbm, wo_hbm, kv_hbm, len_hbm, own_hbm, page_hbm,
    out_ref,
    hid, hid32, wq, wkv, wo, keys, vals, lens, owns, pages,
    q_src, q_rcv, kv_src, kv_rcv, sq_src, sq_rcv, q_all, kv_new,
    sel, sel_t, bias, ownv, acc_src, acc_rcv, st_src, st_rcv, att_all, tp_all,
    local_sem, send_sem, recv_sem,
):
    inst = lax.axis_index("inst")
    tp = lax.axis_index("tp")
    z, x = inst // 4, lax.rem(inst, 4)
    is_owner = z < 4

    def local(i, src, dst):
        return pltpu.make_async_copy(src, dst, local_sem.at[i])

    loads = [
        local(0, hid_hbm, hid),
        local(1, wq_hbm, wq),
        local(2, wk_hbm, wkv.at[:, :HD]),
        local(3, wv_hbm, wkv.at[:, HD:]),
        local(4, own_hbm, owns),
        local(5, page_hbm, pages),
        local(6, len_hbm, lens),
        local(7, kv_hbm.at[0], keys),
        local(8, kv_hbm.at[1], vals),
        local(9, wo_hbm, wo),
    ]
    barrier = pltpu.get_barrier_semaphore()

    @pl.when(is_owner)
    def _():
        @pl.loop(1, N_INST)
        def _(k):
            to = lax.rem(inst + k, N_INST)
            pl.semaphore_signal(barrier, inc=1, device_id={"inst": to}, device_id_type=MESH)

    @pl.loop(1, N_TP)
    def _(k):
        to = lax.rem(tp + k, N_TP)
        pl.semaphore_signal(barrier, inc=1, device_id={"tp": to}, device_id_type=MESH)

    for load in loads:
        load.start()

    def remote(src, dst, i, to):
        return pltpu.make_async_remote_copy(
            src_ref=src, dst_ref=dst, send_sem=send_sem.at[i], recv_sem=recv_sem.at[i],
            device_id=to, device_id_type=MESH,
        )

    def arrived(ref, i):
        pltpu.make_async_copy(ref, ref, recv_sem.at[i]).wait()

    def departed(ref, i):
        pltpu.make_async_copy(ref, ref, send_sem.at[i]).wait()

    def place(owner):
        return lax.rem(inst - owner - 1 + 2 * N_INST, N_INST)

    def to_owners(send):
        @pl.loop(0, OWNERS)
        def _(k):
            zo = lax.rem(k, 4)
            xo = lax.rem(x + far_first(k // 4)[1], 4)
            owner = zo * 4 + xo

            @pl.when(owner != inst)
            def _():
                send(owner)

    def to_all(src, dst, i):
        @pl.loop(0, N_INST - 1)
        def _(k):
            dz, dx = far_first(k)
            to = lax.rem(z + dz, 8) * 4 + lax.rem(x + dx, 4)
            remote(src, dst, i, {"inst": to}).start()

    loads[0].wait()
    for c in range(2):
        hid32[c] = hid[:, HD * c : HD * c + HD].astype(F32)
    rows = jnp.concatenate(
        [
            jnp.concatenate(
                [hid32[c, pl.ds(16 * g + t, 8, stride=2), :] for g in range(4) for t in range(2)], axis=0
            )
            for c in range(2)
        ],
        axis=1,
    )
    squares = jnp.sum(rows * rows, axis=1, keepdims=True)
    spread = jnp.where(iota((64, HD), 0) == iota((64, HD), 1), squares, 0.0)
    sq_src[...] = jnp.sum(spread, axis=0, keepdims=True)
    normed = (rows * gain_ref[...].astype(F32)).astype(BF16)
    loads[1].wait()
    raw = jnp.dot(normed, wq[...], preferred_element_type=F32).astype(BF16)
    for owner in range(OWNERS):
        zo, g = owner // 4, owner % 4
        for k in range(2):
            h = 2 * zo + k
            q_src[owner, 16 * k : 16 * k + 16, :] = raw[16 * g : 16 * g + 16, HD * h : HD * h + HD]
    loads[2].wait()
    loads[3].wait()
    raw = jnp.dot(normed, wkv[...], preferred_element_type=F32).astype(BF16)
    for g in range(4):
        for k in range(2):
            kv_src[g, 16 * k : 16 * k + 16, :] = raw[16 * g : 16 * g + 16, HD * k : HD * k + HD]

    pl.semaphore_wait(barrier, OWNERS + N_TP - 1 - is_owner.astype(jnp.int32))

    def send_query(owner):
        remote(sq_src, sq_rcv.at[place(owner)], 0, {"inst": owner}).start()
        remote(q_src.at[owner], q_rcv.at[place(owner)], 1, {"inst": owner}).start()

    to_owners(send_query)
    for g in range(4):

        @pl.when(inst != g)
        def _():
            remote(kv_src.at[g], kv_rcv.at[place(g)], 2, {"inst": g}).start()

    loads[4].wait()
    loads[5].wait()
    loads[6].wait()
    shifted = iota((16, 512), 1)
    row = iota((16, 512), 0)
    shifted = shifted - ((row // 4) * 128 + (lax.rem(row, 4) // 2) * 16 + lax.rem(row, 2) * 8)

    @pl.loop(0, 32)
    def _(s):
        owner = owns[s]
        safe = jnp.maximum(owner, 0)
        target = jnp.where(owner >= 0, (safe // 8) * 32 + lax.rem(safe, 8), -1000)
        limit = lens[safe] - pages[s] * 256
        sel[pl.ds(pl.multiple_of(16 * s, 16), 16), :] = (shifted == target).astype(F32).astype(BF16)
        bias[pl.ds(s, 1), :] = jnp.where(iota((1, 256), 1) < limit, 0.0, NEG)
        ownv[pl.ds(s, 1), :] = jnp.full((1, HD), owner, jnp.int32)

    sel_t[...] = sel[...].astype(F32).T.astype(BF16)

    @pl.when(is_owner)
    def _():
        spot = iota((16, HD), 0)
        position = jnp.zeros((16, HD), jnp.int32)
        for k in range(8):
            position = jnp.where(lax.rem(spot, 8) == k, lens[8 * x + k], position)
        position = position + spot // 8
        lane = iota((16, HD), 1)
        index = lax.rem(lane, 64).astype(F32)
        angle = position.astype(F32) * jnp.exp(index * (-2.0 / HD * 13.122363377404328))
        cosine = jnp.cos(angle)
        sine = jnp.sin(angle) * jnp.where(lane < 64, -1.0, 1.0)
        arrived(sq_rcv, 0)
        total = jnp.sum(sq_rcv[...], axis=0) + sq_src[...]
        mine = jnp.where(lane == 16 * x + spot, total, 0.0)
        inverse = lax.rsqrt(jnp.sum(mine, axis=1, keepdims=True) / D + EPS)
        arrived(q_rcv, 1)
        joined = jnp.sum(q_rcv[...].astype(F32), axis=0) + q_src[inst].astype(F32)
        for k in range(2):
            part = rope(joined[16 * k : 16 * k + 16] * inverse, cosine, sine)
            q_all[inst, 16 * k : 16 * k + 16, :] = part.astype(BF16)
        to_all(q_all.at[inst], q_all.at[inst], 3)

        @pl.when(z == 0)
        def _():
            arrived(kv_rcv, 2)
            both = jnp.sum(kv_rcv[...].astype(F32), axis=0) + kv_src[inst].astype(F32)
            both = both * jnp.concatenate([inverse, inverse], axis=0)
            kv_new[0:16, :] = rope(both[0:16], cosine, sine).astype(BF16)
            kv_new[16:32, :] = both[16:32].astype(BF16)
            for k in range(1, 4):
                remote(kv_new, kv_new, 4, {"inst": 4 * k + x}).start()

    loads[7].wait()
    loads[8].wait()

    @pl.when(is_owner)
    def _():
        arrived(q_all.at[0:15], 3)

    @pl.when(jnp.logical_not(is_owner))
    def _():
        arrived(q_all, 3)

    queries = jnp.dot(sel[...], q_all[...].reshape(512, HD), preferred_element_type=F32).astype(BF16)
    scores = lax.dot_general(
        queries.reshape(32, 16, HD), keys[...], (((2,), (2,)), ((0,), (0,))), preferred_element_type=F32
    )
    scores = scores * SCALE + bias[...][:, None, :]
    top = jnp.max(scores, axis=2, keepdims=True)
    weights = jnp.exp(scores - top)
    weight_sum = jnp.sum(weights, axis=2, keepdims=True)
    part = lax.dot_general(
        weights.astype(BF16), vals[...], (((2,), (1,)), ((0,), (0,))), preferred_element_type=F32
    )
    diagonal = iota((32, 16, HD), 1) == iota((32, 16, HD), 2)
    top_row = jnp.sum(jnp.where(diagonal, top, 0.0), axis=1)
    sum_row = jnp.sum(jnp.where(diagonal, weight_sum, 0.0), axis=1)
    owner_row = ownv[...]
    same = owner_row[:, None, :] == owner_row[None, :, :]
    peak_row = jnp.max(jnp.where(same, top_row[None, :, :], NEG), axis=1)
    factor = jnp.exp(top_row - peak_row)
    factor_col = jnp.sum(jnp.where(diagonal, factor[:, None, :], 0.0), axis=2, keepdims=True)
    part = (part * factor_col).reshape(512, HD)
    high = part.astype(BF16)
    low = (part - high.astype(F32)).astype(BF16)
    both = jnp.dot(sel_t[...], jnp.concatenate([high, low], axis=1), preferred_element_type=F32)
    acc_src[...] = (both[:, :HD] + both[:, HD:]).astype(BF16).reshape(OWNERS, 32, HD)
    member = owner_row[None, :, :] == iota((32, 32, HD), 0)
    top_req = jnp.max(jnp.where(member, top_row[None, :, :], NEG), axis=1)
    sum_req = jnp.sum(jnp.where(member, (factor * sum_row)[None, :, :], 0.0), axis=1)
    st_src[...] = jnp.where(
        iota((32, HD), 1) < 16, top_req, pltpu.roll(sum_req, 16, 1)
    ).reshape(4, 8, HD)

    def send_parts(owner):
        remote(st_src.at[lax.rem(owner, 4)], st_rcv.at[place(owner)], 5, {"inst": owner}).start()
        remote(acc_src.at[owner], acc_rcv.at[place(owner)], 6, {"inst": owner}).start()

    to_owners(send_parts)

    @pl.when(is_owner)
    def _():
        @pl.when(z > 0)
        def _():
            arrived(kv_new, 4)

        row = iota((32, 16), 0)
        key = iota((32, 16), 1)
        seen = (lax.rem(row, 8) == lax.rem(key, 8)) & (key // 8 <= lax.rem(row, 16) // 8)
        fresh = lax.dot_general(
            q_all[inst], kv_new[0:16, :], (((1,), (1,)), ((), ())), preferred_element_type=F32
        ) * SCALE
        fresh = jnp.where(seen, fresh, NEG)
        fresh_top = jnp.max(fresh, axis=1, keepdims=True)
        weights = jnp.where(seen, jnp.exp(fresh - fresh_top), 0.0)
        fresh_sum = jnp.sum(weights, axis=1, keepdims=True)
        fresh_out = jnp.dot(weights.astype(BF16), kv_new[16:32, :], preferred_element_type=F32)
        lane = iota((8, HD), 1)
        top_lanes = jnp.full((8, HD), NEG, F32)
        sum_lanes = jnp.zeros((8, HD), F32)
        for k in range(4):
            top_lanes = jnp.where(lane == k, fresh_top[8 * k : 8 * k + 8], top_lanes)
            sum_lanes = jnp.where(lane == k, fresh_sum[8 * k : 8 * k + 8], sum_lanes)

        arrived(st_rcv, 5)
        stats = jnp.concatenate([st_rcv[...], st_src[pl.ds(x, 1)]], axis=0).reshape(256, HD)
        tops = pltpu.roll(stats, lax.rem(HD - 4 * z, HD), 1)
        sums = pltpu.roll(tops, HD - 16, 1).reshape(32, 8, HD)
        tops = tops.reshape(32, 8, HD)
        peak = jnp.maximum(jnp.max(tops, axis=0), top_lanes)
        scale = jnp.exp(tops - peak[None])
        fresh_scale = jnp.exp(top_lanes - peak)
        total = jnp.sum(scale * sums, axis=0) + fresh_scale * sum_lanes
        arrived(acc_rcv, 6)
        parts = jnp.concatenate([acc_rcv[...], acc_src[pl.ds(inst, 1)]], axis=0).astype(F32)
        done = []
        for k in range(4):
            out = jnp.sum(parts[:, 8 * k : 8 * k + 8, :] * scale[:, :, k : k + 1], axis=0)
            out = out + fresh_scale[:, k : k + 1] * fresh_out[8 * k : 8 * k + 8]
            done.append(out / total[:, k : k + 1])
        att_all[inst] = jnp.concatenate(done, axis=0).astype(BF16)
        to_all(att_all.at[inst], att_all.at[inst], 7)

    loads[9].wait()

    @pl.when(is_owner)
    def _():
        arrived(att_all.at[0:15], 7)

    @pl.when(jnp.logical_not(is_owner))
    def _():
        arrived(att_all, 7)

    attention = jnp.concatenate(
        [
            jnp.concatenate(
                [att_all[4 * zo + g, 16 * k : 16 * k + 16, :] for zo in range(4) for k in range(2)], axis=1
            )
            for g in range(4)
        ],
        axis=0,
    )
    tp_all[tp] = jnp.dot(attention, wo[...], preferred_element_type=F32).astype(BF16)

    @pl.loop(1, N_TP)
    def _(k):
        to = lax.rem(tp + k, N_TP)
        remote(tp_all.at[tp], tp_all.at[tp], 8, {"tp": to}).start()

    arrived(tp_all.at[0:7], 8)
    mixed = tp_all[0].astype(F32)
    for k in range(1, N_TP):
        mixed = mixed + tp_all[k].astype(F32)
    for g in range(4):
        for t in range(2):
            first = 16 * g + 8 * t
            for c in range(2):
                cols = slice(HD * c, HD * c + HD)
                out_ref[c, pl.ds(16 * g + t, 8, stride=2), :] = mixed[first : first + 8, cols]

    departed(tp_all.at[0:7], 8)

    @pl.when(is_owner)
    def _():
        for i, ref in ((1, q_src), (6, acc_src)):
            departed(ref.at[0:15], i)
        departed(sq_rcv.at[0:15], 0)
        departed(st_rcv.at[0:15], 5)
        departed(q_rcv, 3)
        departed(acc_rcv, 7)

        @pl.when(z == 0)
        def _():
            departed(kv_src.at[0:3], 2)
            departed(kv_src.at[0:3], 4)

        @pl.when(z > 0)
        def _():
            departed(kv_src, 2)

    @pl.when(jnp.logical_not(is_owner))
    def _():
        for i, ref in ((1, q_src), (6, acc_src), (2, kv_src)):
            departed(ref, i)
        departed(sq_rcv.at[0:16], 0)
        departed(st_rcv.at[0:16], 5)


def on_device(
    hidden, norm_gain, w_query, w_key, w_value, w_out, kv_cache, lengths, slot_owner, slot_page
):
    hbm = pl.BlockSpec(memory_space=pl.ANY)
    vmem = pl.BlockSpec(memory_space=pltpu.VMEM)
    mixed = pl.pallas_call(
        kernel,
        out_shape=jax.ShapeDtypeStruct((2, 64, HD), F32),
        in_specs=[hbm, vmem] + [hbm] * 8,
        out_specs=vmem,
        scratch_shapes=[
            pltpu.VMEM((64, 256), BF16),
            pltpu.VMEM((2, 64, HD), F32),
            pltpu.VMEM((256, 1024), BF16),
            pltpu.VMEM((256, 256), BF16),
            pltpu.VMEM((1024, 256), BF16),
            pltpu.VMEM((32, 256, HD), BF16),
            pltpu.VMEM((32, 256, HD), BF16),
            pltpu.SMEM((32,), jnp.int32),
            pltpu.SMEM((32,), jnp.int32),
            pltpu.SMEM((32,), jnp.int32),
            pltpu.VMEM((OWNERS, 32, HD), BF16),
            pltpu.VMEM((31, 32, HD), BF16),
            pltpu.VMEM((4, 32, HD), BF16),
            pltpu.VMEM((31, 32, HD), BF16),
            pltpu.VMEM((1, HD), F32),
            pltpu.VMEM((31, 1, HD), F32),
            pltpu.VMEM((OWNERS, 32, HD), BF16),
            pltpu.VMEM((32, HD), BF16),
            pltpu.VMEM((512, 512), BF16),
            pltpu.VMEM((512, 512), BF16),
            pltpu.VMEM((32, 256), F32),
            pltpu.VMEM((32, HD), jnp.int32),
            pltpu.VMEM((OWNERS, 32, HD), BF16),
            pltpu.VMEM((31, 32, HD), BF16),
            pltpu.VMEM((4, 8, HD), F32),
            pltpu.VMEM((31, 8, HD), F32),
            pltpu.VMEM((OWNERS, 32, HD), BF16),
            pltpu.VMEM((N_TP, 64, 256), BF16),
            pltpu.SemaphoreType.DMA((10,)),
            pltpu.SemaphoreType.DMA((9,)),
            pltpu.SemaphoreType.DMA((9,)),
        ],
        compiler_params=pltpu.CompilerParams(
            collective_id=0, has_side_effects=True, vmem_limit_bytes=40 * 1024 * 1024
        ),
        name="paged_attention",
    )(
        hidden, norm_gain.reshape(1, -1), w_query, w_key, w_value, w_out, kv_cache,
        lengths, slot_owner, slot_page,
    )
    return mixed.transpose(1, 0, 2).reshape(64, 256).astype(BF16)


def solution(mesh):
    return jax.shard_map(
        on_device,
        mesh=mesh,
        in_specs=(
            P(None, "inst"),
            P("inst"),
            P("inst", "tp"),
            P("inst", "tp"),
            P("inst", "tp"),
            P("tp", "inst"),
            P(None, "inst", None, "tp"),
            P(),
            P("inst"),
            P("inst"),
        ),
        out_specs=P(None, "inst"),
        check_vma=False,
    )
```

time: 346 us -> 66 us (0.19)
  blocking collectives: 164 us -> 0 us
  waiting for transfers between devices: 97.8 us -> 0 us
  Pallas kernels: 0 us -> 55.6 us
  local copies, waits for them, and re-layouts: 39.5 us -> 9.33 us
  other arithmetic: 18.2 us -> 0.62 us
  between operations: 13.6 us -> 0.02 us
  matrix products: 9.9 us -> 0 us
    psum x2 -> x0, blocking collectives: 88.1 us -> none  [the longest x1 64.4 us: on_device(): lax.psum((jnp.concatenate([jnp.dot(normed, w_query, preferred_element_typ...]
    all_gather x2 -> x0, blocking collectives: 75.4 us -> none  [joined_2(): everything = jax.tree.map(lambda part: lax.all_gather(part, axis), x)]
    psum x1 -> x0, waiting for transfers between devices: 73.6 us -> none  [on_device(): lax.psum((jnp.concatenate([jnp.dot(normed, w_query, preferred_element_typ...]
    pallas_call x0 -> x1, Pallas kernels: none -> 55.6 us  [on_device(): pl.pallas_call(kernel, out_shape=jax.ShapeDtypeStruct((2, 64, HD), F32),...]
    dynamic_slice x31 -> x0, local copies, waits for them, and re-layouts: 30.2 us -> none  [lap(): return combine(so_far, jax.tree.map(lambda part: part[k], everything))]
    all_gather x1 -> x0, waiting for transfers between devices: 24.2 us -> none  [joined_2(): everything = jax.tree.map(lambda part: lax.all_gather(part, axis), x)]
    add x63 -> x0, other arithmetic: 9.95 us -> none  [the longest x31 9.35 us: join(): scale_first[..., None] * first_part[2]]
    dot_general x10 -> x0, matrix products: 9.9 us -> none  [the longest x2 2.46 us: soft_terms(): jnp.einsum(out_form, weights.astype(jnp.bfloat16), values_block, preferre...]
  transfers between devices with their start and end apart: 2 -> 0, of which waited for: 2 -> 0; matrix products, arithmetic and copies ran while one was open for 2% -> 0% of each run, Pallas kernels for 0% -> 0%
where the time goes in v1:
time: 66 us; the launch traced here: 65.6 us
  Pallas kernels  55.6 us (84%)
  local copies, waits for them, and re-layouts  9.33 us (14%)
    pallas_call x1, Pallas kernels, on_device(): pl.pallas_call(kernel, out_shape=jax.ShapeDtypeStruct((2, 64, HD), F32),...  55.6 us
    unnamed x18, local copies, waits for them, and re-layouts  8.67 us

profile of v1, /device:TPU:1, one launch (start us, length us, event | category | flops | bytes accessed | tf_op | source)
XLA Modules:
  0.0 65.6 jit_solution(14221940319959952090)
XLA Ops:
  0.0 0.7 %reshape.5.gain_ref = bf16[1,256]{1,0:T(2,128)(2,1)S(1)} reshape(bf16[256]{0:T(256)(128)(2,1)} %param.11) | data formatting | bytes 1024 | tf_op jit(solution)/shard_map/reshape | solution.py:416
  0.7 0.0 copy-start
  0.7 2.2 %copy-done = bf16[2,32,256,128]{3,2,1,0:T(8,128)(2,1)S(1)} copy-done((bf16[2,32,256,128]{3,2,1,0:T(8,128)(2,1)S(1)}, bf16[2,32,256,128]{3,2,1,0:T(8,128)(2,1)}, u32[]{:S(2)}) %copy-start) | copy-done | bytes 4194328
  2.8 0.0 copy-start.1
  2.8 1.0 %copy-done.1 = bf16[256,1024]{1,0:T(8,128)(2,1)S(1)} copy-done((bf16[256,1024]{1,0:T(8,128)(2,1)S(1)}, bf16[256,1024]{1,0:T(8,128)(2,1)}, u32[]{:S(2)}) %copy-start.1) | copy-done | bytes 524312
  3.9 0.0 copy-start.2
  3.9 1.0 %copy-done.2 = bf16[1024,256]{1,0:T(8,128)(2,1)S(1)} copy-done((bf16[1024,256]{1,0:T(8,128)(2,1)S(1)}, bf16[1024,256]{1,0:T(8,128)(2,1)}, u32[]{:S(2)}) %copy-start.2) | copy-done | bytes 524312
  4.9 0.0 copy-start.3
  4.9 0.8 %copy-done.3 = bf16[256,128]{1,0:T(8,128)(2,1)S(1)} copy-done((bf16[256,128]{1,0:T(8,128)(2,1)S(1)}, bf16[256,128]{1,0:T(8,128)(2,1)}, u32[]{:S(2)}) %copy-start.3) | copy-done | bytes 65560
  5.8 0.0 copy-start.4
  5.8 0.8 %copy-done.4 = bf16[256,128]{1,0:T(8,128)(2,1)S(1)} copy-done((bf16[256,128]{1,0:T(8,128)(2,1)S(1)}, bf16[256,128]{1,0:T(8,128)(2,1)}, u32[]{:S(2)}) %copy-start.4) | copy-done | bytes 65560
  6.6 0.0 copy-start.5
  6.6 0.8 %copy-done.5 = bf16[64,256]{1,0:T(8,128)(2,1)S(1)} copy-done((bf16[64,256]{1,0:T(8,128)(2,1)S(1)}, bf16[64,256]{1,0:T(8,128)(2,1)}, u32[]{:S(2)}) %copy-start.5) | copy-done | bytes 32792
  7.4 0.0 copy-start.6
  7.4 0.7 copy-done.6
  8.0 0.0 copy-start.7
  8.0 0.7 copy-done.7
  8.7 0.0 copy-start.8
  8.7 0.7 copy-done.8
  9.3 55.6 %paged_attention.1 = f32[2,64,128]{2,1,0:T(8,128)S(1)} custom-call(bf16[64,256]{1,0:T(8,128)(2,1)S(1)} %copy-done.5, bf16[1,256]{1,0:T(2,128)(2,1)S(1)} %reshape.5.gain_ref, bf16[256,1024]{1,0:T(8,128)(2,1)S(1)} %copy-done.1, bf16[256,128]{1,0:T(8,128)(2,1)S(1)} %copy-done.3, bf16[256,128]{1,0:T(8,128)(2,1)S(1)} %copy-done.4, ...), custom_call_target="tpu_custom_call" | custom-call | tf_op jit(solution)/shard_map/paged_attention/pallas_call | solution.py:373
  65.0 0.6 copy_bitcast_fusion
Async XLA Ops:
  0.7 2.2 %copy-start = (bf16[2,32,256,128]{3,2,1,0:T(8,128)(2,1)S(1)}, bf16[2,32,256,128]{3,2,1,0:T(8,128)(2,1)}, u32[]{:S(2)}) copy-start(bf16[2,32,256,128]{3,2,1,0:T(8,128)(2,1)} %kv_hbm.1) | copy-start | bytes 12582916
  2.8 1.0 %copy-start.1 = (bf16[256,1024]{1,0:T(8,128)(2,1)S(1)}, bf16[256,1024]{1,0:T(8,128)(2,1)}, u32[]{:S(2)}) copy-start(bf16[256,1024]{1,0:T(8,128)(2,1)} %wq_hbm.1) | copy-start | bytes 1572868
  3.9 1.0 %copy-start.2 = (bf16[1024,256]{1,0:T(8,128)(2,1)S(1)}, bf16[1024,256]{1,0:T(8,128)(2,1)}, u32[]{:S(2)}) copy-start(bf16[1024,256]{1,0:T(8,128)(2,1)} %wo_hbm.1) | copy-start | bytes 1572868
  4.9 0.8 %copy-start.3 = (bf16[256,128]{1,0:T(8,128)(2,1)S(1)}, bf16[256,128]{1,0:T(8,128)(2,1)}, u32[]{:S(2)}) copy-start(bf16[256,128]{1,0:T(8,128)(2,1)} %wk_hbm.1) | copy-start | bytes 196612
  5.8 0.8 %copy-start.4 = (bf16[256,128]{1,0:T(8,128)(2,1)S(1)}, bf16[256,128]{1,0:T(8,128)(2,1)}, u32[]{:S(2)}) copy-start(bf16[256,128]{1,0:T(8,128)(2,1)} %wv_hbm.1) | copy-start | bytes 196612
  6.6 0.8 %copy-start.5 = (bf16[64,256]{1,0:T(8,128)(2,1)S(1)}, bf16[64,256]{1,0:T(8,128)(2,1)}, u32[]{:S(2)}) copy-start(bf16[64,256]{1,0:T(8,128)(2,1)} %hid_hbm.1) | copy-start | bytes 98308
  7.4 0.7 copy-start.6
  8.0 0.7 copy-start.7
  8.7 0.7 copy-start.8

commit v2 on v1

v2 whole, which is shorter than its diff:
```python
import functools

import jax
import jax.numpy as jnp
from jax import lax
from jax.experimental import pallas as pl
from jax.experimental.pallas import tpu as pltpu
from jax.sharding import PartitionSpec as P

D = 8192
HD = 128
NEG = -1e30
EPS = 1e-05
THETA = 500000.0
SCALE = HD ** -0.5
N_INST = 32
N_TP = 8
MESH = pl.DeviceIdType.MESH
F32 = jnp.float32
BF16 = jnp.bfloat16


def iota(shape, dim):
    return lax.broadcasted_iota(jnp.int32, shape, dim)


def far_first():
    offsets = [(dz, dx) for dz in range(8) for dx in range(4) if dz or dx]
    return sorted(offsets, key=lambda o: -min(o[0], 8 - o[0]) - min(o[1], 4 - o[1]))


def rope(rows, cosine, sine):
    return rows * cosine + pltpu.roll(rows, 64, 1) * sine


def kernel(
    hid_hbm, gain_hbm, wq_hbm, wk_hbm, wv_hbm, wo_hbm, kv_hbm, len_hbm, own_hbm, page_hbm,
    out_ref,
    hid, hid32, gain, wq, wkv, wo, keys, vals, lens, owns, pages,
    q_src, q_rcv, kv_src, kv_rcv, sq_src, sq_rcv, q_all, kv_new,
    sel, sel_t, bias, member, acc_src, acc_rcv, st_src, st_rcv, att_all, tp_all,
    local_sem, send_sem, recv_sem,
):
    inst = lax.axis_index("inst")
    tp = lax.axis_index("tp")
    z, x = inst // 4, lax.rem(inst, 4)
    peers = [
        lax.rem(z + dz, 8) * 4 + lax.rem(x + dx, 4) for dz, dx in far_first()
    ]
    tp_peers = [lax.rem(tp + k, N_TP) for k in (4, 5, 3, 2, 6, 1, 7)]

    def local(i, src, dst):
        return pltpu.make_async_copy(src, dst, local_sem.at[i])

    loads = [
        local(0, hid_hbm, hid),
        local(1, wq_hbm, wq),
        local(2, wk_hbm, wkv.at[:, :HD]),
        local(3, wv_hbm, wkv.at[:, HD:]),
        local(4, own_hbm, owns),
        local(5, page_hbm, pages),
        local(6, len_hbm, lens),
        local(7, kv_hbm.at[0], keys),
        local(8, kv_hbm.at[1], vals),
        local(9, wo_hbm, wo),
        local(10, gain_hbm, gain),
    ]
    barrier = pltpu.get_barrier_semaphore()
    for to in peers:
        pl.semaphore_signal(barrier, inc=1, device_id={"inst": to}, device_id_type=MESH)
    for to in tp_peers:
        pl.semaphore_signal(barrier, inc=1, device_id={"tp": to}, device_id_type=MESH)
    for load in [loads[0], loads[10]] + loads[1:10]:
        load.start()

    def remote(src, dst, i, to):
        return pltpu.make_async_remote_copy(
            src_ref=src, dst_ref=dst, send_sem=send_sem.at[i], recv_sem=recv_sem.at[i],
            device_id=to, device_id_type=MESH,
        )

    def arrived(ref, i):
        pltpu.make_async_copy(ref, ref, recv_sem.at[i]).wait()

    def departed(ref, i):
        pltpu.make_async_copy(ref, ref, send_sem.at[i]).wait()

    def drain(stage):
        if stage > 0:
            departed(sq_rcv, 0)
            departed(q_rcv, 1)

            @pl.when(z == 0)
            def _():
                departed(kv_src.at[0:3], 2)

            @pl.when(z > 0)
            def _():
                departed(kv_src, 2)

        if stage > 1:
            departed(q_rcv, 3)

            @pl.when(z == 0)
            def _():
                departed(kv_rcv.at[0:7], 4)

        if stage > 2:
            departed(st_rcv, 5)
            departed(acc_rcv, 6)
        if stage > 3:
            departed(acc_rcv, 7)
            departed(tp_all.at[0:7], 8)

    def place(to):
        return lax.rem(inst - to + (N_INST - 1), N_INST)

    places = [place(to) for to in peers]

    def to_all(src, dst, i):
        for to in peers:
            remote(src, dst, i, {"inst": to}).start()

    loads[0].wait()
    for c in range(2):
        hid32[c] = hid[:, HD * c : HD * c + HD].astype(F32)
    rows = jnp.concatenate(
        [
            jnp.concatenate(
                [hid32[c, pl.ds(16 * g + t, 8, stride=2), :] for g in range(4) for t in range(2)], axis=0
            )
            for c in range(2)
        ],
        axis=1,
    )
    squares = jnp.sum(rows * rows, axis=1, keepdims=True)
    spread = jnp.where(iota((64, HD), 0) == iota((64, HD), 1), squares, 0.0)
    sq_src[...] = jnp.sum(spread, axis=0, keepdims=True)
    loads[10].wait()
    normed = (rows * gain[...].astype(F32).reshape(1, 256)).astype(BF16)
    loads[1].wait()
    raw = jnp.dot(normed, wq[...], preferred_element_type=F32).astype(BF16)
    for h in range(8):
        for g in range(4):
            q_src[4 * h + g] = raw[16 * g : 16 * g + 16, HD * h : HD * h + HD]
    loads[2].wait()
    loads[3].wait()
    raw = jnp.dot(normed, wkv[...], preferred_element_type=F32).astype(BF16)
    for g in range(4):
        for k in range(2):
            kv_src[g, 16 * k : 16 * k + 16, :] = raw[16 * g : 16 * g + 16, HD * k : HD * k + HD]

    pl.semaphore_wait(barrier, N_INST - 1 + N_TP - 1)

    for to, there in zip(peers, places):
        remote(q_src.at[to], q_rcv.at[there], 1, {"inst": to}).start()
        remote(sq_src, sq_rcv.at[there], 0, {"inst": to}).start()
    for g in range(4):

        @pl.when(inst != g)
        def _():
            remote(kv_src.at[g], kv_rcv.at[place(g)], 2, {"inst": g}).start()

    loads[6].wait()
    spot = iota((16, HD), 0)
    lane = iota((16, HD), 1)
    position = jnp.zeros((16, HD), jnp.int32)
    for k in range(8):
        position = jnp.where(lax.rem(spot, 8) == k, lens[8 * x + k], position)
    position = position + spot // 8
    index = lax.rem(lane, 64).astype(F32)
    angle = position.astype(F32) * jnp.exp(index * (-2.0 / HD * 13.122363377404328))
    cosine = jnp.cos(angle)
    sine = jnp.sin(angle) * jnp.where(lane < 64, -1.0, 1.0)

    arrived(sq_rcv, 0)
    total = jnp.sum(sq_rcv[...], axis=0) + sq_src[...]
    mine = jnp.where(lane == 16 * x + spot, total, 0.0)
    inverse = lax.rsqrt(jnp.sum(mine, axis=1, keepdims=True) / D + EPS)
    arrived(q_rcv, 1)
    joined = jnp.sum(q_rcv[...].astype(F32), axis=0) + q_src[inst].astype(F32)
    q_all[inst] = rope(joined * inverse, cosine, sine).astype(BF16)
    to_all(q_all.at[inst], q_all.at[inst], 3)

    loads[4].wait()
    loads[5].wait()
    row = iota((16, 512), 0)
    shifted = iota((16, 512), 1) - ((row // 2) * 64 + lax.rem(row, 2) * 8)
    column = iota((1, 512), 1)

    def slot(s, targets):
        owner = owns[s]
        safe = jnp.maximum(owner, 0)
        target = jnp.where(owner >= 0, (safe // 8) * 16 + lax.rem(safe, 8), -1000)
        limit = jnp.where(owner >= 0, lens[safe] - pages[s] * 256, 0)
        sel[pl.ds(pl.multiple_of(16 * s, 16), 16), :] = (shifted == target).astype(F32).astype(BF16)
        bias[s] = jnp.where(iota((1, 256), 1) < limit, 0.0, NEG)
        member[s] = (iota((1, HD), 1) == owner).astype(jnp.int32)
        return jnp.where(column // 16 == s, target, targets)

    targets = lax.fori_loop(0, 32, slot, jnp.zeros((1, 512), jnp.int32), unroll=4)
    j = lax.rem(column, 16)
    targets = targets + (j // 2) * 64 + lax.rem(j, 2) * 8
    sel_t[...] = (iota((512, 512), 0) == targets).astype(F32).astype(BF16)

    @pl.when(z == 0)
    def _():
        arrived(kv_rcv, 2)
        both = jnp.sum(kv_rcv[...].astype(F32), axis=0) + kv_src[inst].astype(F32)
        both = both * jnp.concatenate([inverse, inverse], axis=0)
        kv_new[0:16, :] = rope(both[0:16], cosine, sine).astype(BF16)
        kv_new[16:32, :] = both[16:32].astype(BF16)
        for k in range(1, 8):
            remote(kv_new, kv_new, 4, {"inst": 4 * k + x}).start()

    loads[7].wait()
    loads[8].wait()
    arrived(q_all.at[0:31], 3)
    queries = jnp.dot(sel[...], q_all[...].reshape(512, HD), preferred_element_type=F32).astype(BF16)
    scores = lax.dot_general(
        queries.reshape(32, 16, HD), keys[...], (((2,), (2,)), ((0,), (0,))), preferred_element_type=F32
    )
    scores = scores * SCALE + bias[...]
    top = jnp.max(scores, axis=2, keepdims=True)
    weights = jnp.exp(scores - top)
    weight_sum = jnp.sum(weights, axis=2, keepdims=True)
    part = lax.dot_general(
        weights.astype(BF16), vals[...], (((2,), (1,)), ((0,), (0,))), preferred_element_type=F32
    )
    belongs = member[...] > 0
    top_req = jnp.max(jnp.where(belongs, top, NEG), axis=0)
    peak = jnp.max(jnp.where(belongs, top_req[None], NEG), axis=2, keepdims=True)
    factor = jnp.exp(top - peak)
    sum_req = jnp.sum(jnp.where(belongs, factor * weight_sum, 0.0), axis=0)
    stats = jnp.where(iota((16, HD), 1) < 32, top_req, pltpu.roll(sum_req, 32, 1))
    st_src[...] = stats.reshape(8, 2, HD)
    part = (part * factor).reshape(512, HD)
    high = part.astype(BF16)
    low = (part - high.astype(F32)).astype(BF16)
    both = jnp.dot(sel_t[...], jnp.concatenate([high, low], axis=1), preferred_element_type=F32)
    acc_src[...] = (both[:, :HD] + both[:, HD:]).astype(BF16).reshape(N_INST, 16, HD)

    for to, there in zip(peers, places):
        remote(acc_src.at[to], acc_rcv.at[there], 6, {"inst": to}).start()
        remote(st_src.at[to // 4], st_rcv.at[there], 5, {"inst": to}).start()

    @pl.when(z > 0)
    def _():
        arrived(kv_new, 4)

    row = iota((16, 16), 0)
    key = iota((16, 16), 1)
    seen = (lax.rem(row, 8) == lax.rem(key, 8)) & (key // 8 <= row // 8)
    fresh = lax.dot_general(
        q_all[inst], kv_new[0:16, :], (((1,), (1,)), ((), ())), preferred_element_type=F32
    ) * SCALE
    fresh = jnp.where(seen, fresh, NEG)
    fresh_top = jnp.max(fresh, axis=1, keepdims=True)
    weights = jnp.where(seen, jnp.exp(fresh - fresh_top), 0.0)
    fresh_sum = jnp.sum(weights, axis=1, keepdims=True)
    fresh_out = jnp.dot(weights.astype(BF16), kv_new[16:32, :], preferred_element_type=F32)

    arrived(st_rcv, 5)
    own = st_src[pl.ds(z, 1)]
    stats = jnp.concatenate(
        [st_rcv[:, 0, :], own[:, 0, :], st_rcv[:, 1, :], own[:, 1, :]], axis=0
    )
    stats = pltpu.roll(stats, lax.rem(HD - 8 * x, HD), 1).T
    tops, sums = stats[0:8], stats[32:40]
    scales, fresh_scales, totals = [], [], []
    for t in range(2):
        first = fresh_top[8 * t : 8 * t + 8]
        held = tops[:, 32 * t : 32 * t + 32]
        peak = jnp.maximum(jnp.max(held, axis=1, keepdims=True), first)
        scale = jnp.exp(held - peak)
        fresh_scale = jnp.exp(first - peak)
        total = jnp.sum(scale * sums[:, 32 * t : 32 * t + 32], axis=1, keepdims=True)
        totals.append(total + fresh_scale * fresh_sum[8 * t : 8 * t + 8])
        scales.append(scale)
        fresh_scales.append(fresh_scale)
    scale = jnp.concatenate(scales, axis=0)
    arrived(acc_rcv, 6)
    out = jnp.concatenate(fresh_scales, axis=0) * fresh_out
    for d in range(N_INST):
        held = acc_rcv[d] if d < N_INST - 1 else acc_src[inst]
        out = out + scale[:, d : d + 1] * held.astype(F32)
    att_all[inst] = (out / jnp.concatenate(totals, axis=0)).astype(BF16)
    to_all(att_all.at[inst], att_all.at[inst], 7)

    loads[9].wait()
    arrived(att_all.at[0:31], 7)
    attention = jnp.concatenate(
        [jnp.concatenate([att_all[4 * h + g] for h in range(8)], axis=1) for g in range(4)], axis=0
    )
    tp_all[tp] = jnp.dot(attention, wo[...], preferred_element_type=F32).astype(BF16)
    for to in tp_peers:
        remote(tp_all.at[tp], tp_all.at[tp], 8, {"tp": to}).start()
    arrived(tp_all.at[0:7], 8)
    mixed = tp_all[0].astype(F32)
    for k in range(1, N_TP):
        mixed = mixed + tp_all[k].astype(F32)
    for g in range(4):
        for t in range(2):
            first = 16 * g + 8 * t
            for c in range(2):
                cols = slice(HD * c, HD * c + HD)
                out_ref[c, pl.ds(16 * g + t, 8, stride=2), :] = mixed[first : first + 8, cols]

    drain(4)


def on_device(
    hidden, norm_gain, w_query, w_key, w_value, w_out, kv_cache, lengths, slot_owner, slot_page
):
    hbm = pl.BlockSpec(memory_space=pltpu.HBM)
    vmem = pl.BlockSpec(memory_space=pltpu.VMEM)
    mixed = pl.pallas_call(
        kernel,
        out_shape=jax.ShapeDtypeStruct((2, 64, HD), F32),
        in_specs=[hbm] * 10,
        out_specs=vmem,
        scratch_shapes=[
            pltpu.VMEM((64, 256), BF16),
            pltpu.VMEM((2, 64, HD), F32),
            pltpu.VMEM((256,), BF16),
            pltpu.VMEM((256, 1024), BF16),
            pltpu.VMEM((256, 256), BF16),
            pltpu.VMEM((1024, 256), BF16),
            pltpu.VMEM((32, 256, HD), BF16),
            pltpu.VMEM((32, 256, HD), BF16),
            pltpu.SMEM((32,), jnp.int32),
            pltpu.SMEM((32,), jnp.int32),
            pltpu.SMEM((32,), jnp.int32),
            pltpu.VMEM((N_INST, 16, HD), BF16),
            pltpu.VMEM((31, 16, HD), BF16),
            pltpu.VMEM((4, 32, HD), BF16),
            pltpu.VMEM((31, 32, HD), BF16),
            pltpu.VMEM((1, HD), F32),
            pltpu.VMEM((31, 1, HD), F32),
            pltpu.VMEM((N_INST, 16, HD), BF16),
            pltpu.VMEM((32, HD), BF16),
            pltpu.VMEM((512, 512), BF16),
            pltpu.VMEM((512, 512), BF16),
            pltpu.VMEM((32, 1, 256), F32),
            pltpu.VMEM((32, 1, HD), jnp.int32),
            pltpu.VMEM((N_INST, 16, HD), BF16),
            pltpu.VMEM((31, 16, HD), BF16),
            pltpu.VMEM((8, 2, HD), F32),
            pltpu.VMEM((31, 2, HD), F32),
            pltpu.VMEM((N_INST, 16, HD), BF16),
            pltpu.VMEM((N_TP, 64, 256), BF16),
            pltpu.SemaphoreType.DMA((11,)),
            pltpu.SemaphoreType.DMA((9,)),
            pltpu.SemaphoreType.DMA((9,)),
        ],
        compiler_params=pltpu.CompilerParams(
            collective_id=0, has_side_effects=True, vmem_limit_bytes=60 * 1024 * 1024
        ),
        name="paged_attention",
    )(
        hidden, norm_gain, w_query, w_key, w_value, w_out, kv_cache,
        lengths, slot_owner, slot_page,
    )
    return mixed.transpose(1, 0, 2).reshape(64, 256).astype(BF16)


def solution(mesh):
    return jax.shard_map(
        on_device,
        mesh=mesh,
        in_specs=(
            P(None, "inst"),
            P("inst"),
            P("inst", "tp"),
            P("inst", "tp"),
            P("inst", "tp"),
            P("tp", "inst"),
            P(None, "inst", None, "tp"),
            P(),
            P("inst"),
            P("inst"),
        ),
        out_specs=P(None, "inst"),
        check_vma=False,
    )
```

time: 66 us -> 46.8 us (0.71)
  Pallas kernels: 55.6 us -> 45.2 us
  local copies, waits for them, and re-layouts: 9.33 us -> 0 us
  other arithmetic: 0.62 us -> 1.46 us
    pallas_call x1, Pallas kernels: 55.6 us -> 45.2 us  [on_device(): pl.pallas_call(kernel, out_shape=jax.ShapeDtypeStruct((2, 64, HD), F32),...]
    unnamed x18 -> x0, local copies, waits for them, and re-layouts: 8.67 us -> none
    convert_element_type x1, other arithmetic: 0.62 us -> 1.46 us  [on_device(): return mixed.transpose(1, 0, 2).reshape(64, 256).astype(BF16)]
where the time goes in v2:
time: 46.8 us; the launch traced here: 46.7 us
  Pallas kernels  45.2 us (97%)
  other arithmetic  1.46 us (3%)
    pallas_call x1, Pallas kernels, on_device(): pl.pallas_call(kernel, out_shape=jax.ShapeDtypeStruct((2, 64, HD), F32),...  45.2 us
    convert_element_type x1, other arithmetic, on_device(): return mixed.transpose(1, 0, 2).reshape(64, 256).astype(BF16)  1.46 us

profile of v2, /device:TPU:1, one launch (start us, length us, event | category | flops | bytes accessed | tf_op | source)
XLA Modules:
  0.0 46.7 jit_solution(13821853121817212910)
XLA Ops:
  0.0 45.2 %paged_attention.1 = f32[2,64,128]{2,1,0:T(8,128)} custom-call(bf16[64,256]{1,0:T(8,128)(2,1)} %hid_hbm.1, bf16[256]{0:T(256)(128)(2,1)} %gain_hbm.1, bf16[256,1024]{1,0:T(8,128)(2,1)} %wq_hbm.1, bf16[256,128]{1,0:T(8,128)(2,1)} %wk_hbm.1, bf16[256,128]{1,0:T(8,128)(2,1)} %wv_hbm.1, bf16[1024,256]{1,0:T(8,128)(2,1)} %wo_hbm.1, ...), custom_call_target="tpu_custom_call" | custom-call | tf_op jit(solution)/shard_map/paged_attention/pallas_call | solution.py:317
  45.2 1.5 %copy_bitcast_fusion = bf16[64,256]{1,0:T(8,128)(2,1)} fusion(f32[2,64,128]{2,1,0:T(8,128)} %paged_attention.1), kind=kLoop, calls=%fused_computation | loop fusion | flops 16384 | bytes 98304 | tf_op jit(solution)/shard_map/convert_element_type | solution.py:364

commit v3 on v2

--- a/solution.py
+++ b/solution.py
@@ -73,9 +73,10 @@
     for load in [loads[0], loads[10]] + loads[1:10]:
         load.start()
 
-    def remote(src, dst, i, to):
+    def remote(src, dst, i, to, into=None):
+        into = i if into is None else into
         return pltpu.make_async_remote_copy(
-            src_ref=src, dst_ref=dst, send_sem=send_sem.at[i], recv_sem=recv_sem.at[i],
+            src_ref=src, dst_ref=dst, send_sem=send_sem.at[i], recv_sem=recv_sem.at[into],
             device_id=to, device_id_type=MESH,
         )
 
@@ -116,10 +117,6 @@
         return lax.rem(inst - to + (N_INST - 1), N_INST)
 
     places = [place(to) for to in peers]
-
-    def to_all(src, dst, i):
-        for to in peers:
-            remote(src, dst, i, {"inst": to}).start()
 
     loads[0].wait()
     for c in range(2):
@@ -180,7 +177,8 @@
     arrived(q_rcv, 1)
     joined = jnp.sum(q_rcv[...].astype(F32), axis=0) + q_src[inst].astype(F32)
     q_all[inst] = rope(joined * inverse, cosine, sine).astype(BF16)
-    to_all(q_all.at[inst], q_all.at[inst], 3)
+    for to in peers:
+        remote(q_all.at[inst], q_all.at[inst], 3, {"inst": to}).start()
 
     loads[4].wait()
     loads[5].wait()
@@ -201,7 +199,8 @@
     targets = lax.fori_loop(0, 32, slot, jnp.zeros((1, 512), jnp.int32), unroll=4)
     j = lax.rem(column, 16)
     targets = targets + (j // 2) * 64 + lax.rem(j, 2) * 8
-    sel_t[...] = (iota((512, 512), 0) == targets).astype(F32).astype(BF16)
+    turned = lax.rem(iota((512, 512), 0) + 64 * lax.rem(z + 2, 8), 512)
+    sel_t[...] = (turned == targets).astype(F32).astype(BF16)
 
     @pl.when(z == 0)
     def _():
@@ -237,12 +236,26 @@
     part = (part * factor).reshape(512, HD)
     high = part.astype(BF16)
     low = (part - high.astype(F32)).astype(BF16)
-    both = jnp.dot(sel_t[...], jnp.concatenate([high, low], axis=1), preferred_element_type=F32)
-    acc_src[...] = (both[:, :HD] + both[:, HD:]).astype(BF16).reshape(N_INST, 16, HD)
-
-    for to, there in zip(peers, places):
-        remote(acc_src.at[to], acc_rcv.at[there], 6, {"inst": to}).start()
-        remote(st_src.at[to // 4], st_rcv.at[there], 5, {"inst": to}).start()
+    parts = jnp.concatenate([high, low], axis=1)
+
+    def send_stats(dz, dx):
+        to = lax.rem(z + dz, 8) * 4 + lax.rem(x + dx, 4)
+        remote(st_src.at[lax.rem(z + dz, 8)], st_rcv.at[place(to)], 5, {"inst": to}).start()
+
+    def send_part(dz, dx):
+        to = lax.rem(z + dz, 8) * 4 + lax.rem(x + dx, 4)
+        held = acc_src.at[4 * ((dz - 2) % 8) + lax.rem(x + dx, 4)]
+        remote(held, acc_rcv.at[place(to)], 6, {"inst": to}).start()
+
+    for half in range(2):
+        rows = slice(256 * half, 256 * half + 256)
+        both = jnp.dot(sel_t[rows, :], parts, preferred_element_type=F32)
+        both = (both[:, :HD] + both[:, HD:]).astype(BF16)
+        acc_src[16 * half : 16 * half + 16] = both.reshape(16, 16, HD)
+        for dz, dx in far_first():
+            if ((dz - 2) % 8 >= 4) == half:
+                send_part(dz, dx)
+                send_stats(dz, dx)
 
     @pl.when(z > 0)
     def _():
@@ -282,41 +295,42 @@
     arrived(acc_rcv, 6)
     out = jnp.concatenate(fresh_scales, axis=0) * fresh_out
     for d in range(N_INST):
-        held = acc_rcv[d] if d < N_INST - 1 else acc_src[inst]
+        held = acc_rcv[d] if d < N_INST - 1 else acc_src[24 + x]
         out = out + scale[:, d : d + 1] * held.astype(F32)
-    att_all[inst] = (out / jnp.concatenate(totals, axis=0)).astype(BF16)
-    to_all(att_all.at[inst], att_all.at[inst], 7)
+    att_all[x, z] = (out / jnp.concatenate(totals, axis=0)).astype(BF16)
+    for k in range(N_INST - 1):
+        to = k + (k >= inst).astype(jnp.int32)
+        group = lax.rem(x - lax.rem(to, 4) + 4, 4)
+        remote(att_all.at[x, z], att_all.at[x, z], 7, {"inst": to}, 7 + group).start()
 
     loads[9].wait()
-    arrived(att_all.at[0:31], 7)
-    attention = jnp.concatenate(
-        [jnp.concatenate([att_all[4 * h + g] for h in range(8)], axis=1) for g in range(4)], axis=0
-    )
-    tp_all[tp] = jnp.dot(attention, wo[...], preferred_element_type=F32).astype(BF16)
-    for to in tp_peers:
-        remote(tp_all.at[tp], tp_all.at[tp], 8, {"tp": to}).start()
-    arrived(tp_all.at[0:7], 8)
-    mixed = tp_all[0].astype(F32)
-    for k in range(1, N_TP):
-        mixed = mixed + tp_all[k].astype(F32)
-    for g in range(4):
+    for k in (0, 1, 3, 2):
+        g = lax.rem(x + k, 4)
+        arrived(att_all.at[g] if k else att_all.at[g, 0:7], 7 + k)
+        attention = jnp.concatenate([att_all[g, h] for h in range(8)], axis=1)
+        tp_all[tp, g] = jnp.dot(attention, wo[...], preferred_element_type=F32).astype(BF16)
+        for to in tp_peers:
+            remote(tp_all.at[tp, g], tp_all.at[tp, g], 8, {"tp": to}, 11 + k).start()
+    for k in (0, 1, 3, 2):
+        g = lax.rem(x + k, 4)
+        arrived(tp_all.at[0:7, g], 11 + k)
+        mixed = tp_all[0, g].astype(F32)
+        for d in range(1, N_TP):
+            mixed = mixed + tp_all[d, g].astype(F32)
         for t in range(2):
-            first = 16 * g + 8 * t
             for c in range(2):
-                cols = slice(HD * c, HD * c + HD)
-                out_ref[c, pl.ds(16 * g + t, 8, stride=2), :] = mixed[first : first + 8, cols]
+                held = mixed[8 * t : 8 * t + 8, HD * c : HD * c + HD]
+                out_ref[c, g, pl.ds(t, 8, stride=2), :] = held
 
     drain(4)
 
 
-def on_device(
-    hidden, norm_gain, w_query, w_key, w_value, w_out, kv_cache, lengths, slot_owner, slot_page
-):
+def on_device(*arrays):
     hbm = pl.BlockSpec(memory_space=pltpu.HBM)
     vmem = pl.BlockSpec(memory_space=pltpu.VMEM)
     mixed = pl.pallas_call(
         kernel,
-        out_shape=jax.ShapeDtypeStruct((2, 64, HD), F32),
+        out_shape=pltpu.VMEM((2, 4, 16, HD), F32),
         in_specs=[hbm] * 10,
         out_specs=vmem,
         scratch_shapes=[
@@ -347,21 +361,18 @@
             pltpu.VMEM((31, 16, HD), BF16),
             pltpu.VMEM((8, 2, HD), F32),
             pltpu.VMEM((31, 2, HD), F32),
-            pltpu.VMEM((N_INST, 16, HD), BF16),
-            pltpu.VMEM((N_TP, 64, 256), BF16),
+            pltpu.VMEM((4, 8, 16, HD), BF16),
+            pltpu.VMEM((N_TP, 4, 16, 256), BF16),
             pltpu.SemaphoreType.DMA((11,)),
             pltpu.SemaphoreType.DMA((9,)),
-            pltpu.SemaphoreType.DMA((9,)),
+            pltpu.SemaphoreType.DMA((15,)),
         ],
         compiler_params=pltpu.CompilerParams(
-            collective_id=0, has_side_effects=True, vmem_limit_bytes=60 * 1024 * 1024
+            collective_id=0, has_side_effects=True, vmem_limit_bytes=48 * 1024 * 1024
         ),
         name="paged_attention",
-    )(
-        hidden, norm_gain, w_query, w_key, w_value, w_out, kv_cache,
-        lengths, slot_owner, slot_page,
-    )
-    return mixed.transpose(1, 0, 2).reshape(64, 256).astype(BF16)
+    )(*(pltpu.with_memory_space_constraint(a, pltpu.HBM) for a in arrays))
+    return mixed.transpose(1, 2, 0, 3).reshape(64, 256).astype(BF16)
 
 
 def solution(mesh):

time: 46.8 us -> 44.5 us (0.951)
  Pallas kernels: 45.2 us -> 43.7 us
  other arithmetic: 1.46 us -> 0.01 us
  local copies, waits for them, and re-layouts: 0 us -> 0.66 us
    pallas_call x1, Pallas kernels: 45.2 us -> 43.7 us  [on_device(): pl.pallas_call(kernel, out_shape=pltpu.VMEM((2, 4, 16, HD), F32), in_spec...]
    convert_element_type x1, other arithmetic: 1.46 us -> 0.01 us  [on_device(): return mixed.transpose(1, 2, 0, 3).reshape(64, 256).astype(BF16)]
    unnamed x0 -> x1, local copies, waits for them, and re-layouts: none -> 0.62 us
where the time goes in v3:
time: 44.5 us; the launch traced here: 44.4 us
  Pallas kernels  43.7 us (98%)
  local copies, waits for them, and re-layouts  0.66 us (1%)
    pallas_call x1, Pallas kernels, on_device(): pl.pallas_call(kernel, out_shape=pltpu.VMEM((2, 4, 16, HD), F32), in_spec...  43.7 us

profile of v3, /device:TPU:1, one launch (start us, length us, event | category | flops | bytes accessed | tf_op | source)
XLA Modules:
  0.0 44.4 jit_solution(8277007773808312511)
XLA Ops:
  0.0 43.7 %paged_attention.1 = f32[2,4,16,128]{3,2,1,0:T(8,128)S(1)} custom-call(bf16[64,256]{1,0:T(8,128)(2,1)} %hid_hbm.1, bf16[256]{0:T(256)(128)(2,1)} %gain_hbm.1, bf16[256,1024]{1,0:T(8,128)(2,1)} %wq_hbm.1, bf16[256,128]{1,0:T(8,128)(2,1)} %wk_hbm.1, bf16[256,128]{1,0:T(8,128)(2,1)} %wv_hbm.1, bf16[1024,256]{1,0:T(8,128)(2,1)} %wo_hbm.1, ...), custom_call_target="tpu_custom_call" | custom-call | tf_op jit(solution)/shard_map/paged_attention/pallas_call | solution.py:331
  43.8 0.6 %copy.14 = bf16[8,8,2,128]{3,1,2,0:T(8,128)(2,1)} copy(bf16[8,8,2,128]{3,2,1,0:T(2,128)(2,1)S(1)} %bitcast.7) | data formatting | bytes 65536
  (2 shorter events, 0.0 us)

commit v4 on v3

v4 whole, which is shorter than its diff:
```python
import functools

import jax
import jax.numpy as jnp
from jax import lax
from jax.experimental import pallas as pl
from jax.experimental.pallas import tpu as pltpu
from jax.sharding import PartitionSpec as P

D = 8192
HD = 128
NEG = -1e30
EPS = 1e-05
THETA = 500000.0
SCALE = HD ** -0.5
N_INST = 32
N_TP = 8
MESH = pl.DeviceIdType.MESH
F32 = jnp.float32
BF16 = jnp.bfloat16


def iota(shape, dim):
    return lax.broadcasted_iota(jnp.int32, shape, dim)


def far_first():
    offsets = [(dz, dx) for dz in range(8) for dx in range(4) if dz or dx]
    return sorted(offsets, key=lambda o: -min(o[0], 8 - o[0]) - min(o[1], 4 - o[1]))


def rope(rows, cosine, sine):
    return rows * cosine + pltpu.roll(rows, 64, 1) * sine


def kernel(
    hid_hbm, gain_hbm, wq_hbm, wk_hbm, wv_hbm, wo_hbm, kv_hbm, len_hbm, own_hbm, page_hbm,
    out_ref,
    hid, hid32, gain, wq, wkv, wo, keys, vals, lens, owns, pages,
    q_src, q_rcv, kv_src, kv_rcv, sq_src, sq_rcv, q_all, q_low, kv_new,
    sel, sel_t, bias, member, acc_src, acc_rcv, st_src, st_rcv, att_all, tp_all,
    local_sem, send_sem, recv_sem,
):
    inst = lax.axis_index("inst")
    tp = lax.axis_index("tp")
    z, x = inst // 4, lax.rem(inst, 4)
    core, y = lax.rem(tp, 2), tp // 2
    low = tp - core
    high = low + 1
    is_low, is_high = core == 0, core == 1
    offsets = far_first()
    peers = [lax.rem(z + dz, 8) * 4 + lax.rem(x + dx, 4) for dz, dx in offsets]
    tp_peers = [lax.rem(tp + k, N_TP) for k in (4, 5, 3, 2, 6, 1, 7)]

    def local(i, src, dst):
        return pltpu.make_async_copy(src, dst, local_sem.at[i])

    loads = [
        local(0, hid_hbm, hid),
        local(1, wq_hbm, wq),
        local(2, wk_hbm, wkv.at[:, :HD]),
        local(3, wv_hbm, wkv.at[:, HD:]),
        local(4, own_hbm, owns),
        local(5, page_hbm, pages),
        local(6, len_hbm, lens),
        local(7, kv_hbm.at[0], keys),
        local(8, kv_hbm.at[1], vals),
        local(9, wo_hbm, wo.at[1]),
        local(10, gain_hbm, gain),
    ]
    barrier = pltpu.get_barrier_semaphore()

    def greet(to):
        pl.semaphore_signal(barrier, inc=1, device_id=to, device_id_type=MESH)

    @pl.when(is_high)
    def _():
        for to in peers:
            greet({"inst": to, "tp": tp})
            greet({"inst": to, "tp": low})

    for to in tp_peers:
        greet({"inst": inst, "tp": to})
    for load in [loads[0], loads[10]] + loads[1:9]:
        load.start()

    def remote(src, dst, i, to, into):
        return pltpu.make_async_remote_copy(
            src_ref=src, dst_ref=dst, send_sem=send_sem.at[i], recv_sem=recv_sem.at[into],
            device_id=to, device_id_type=MESH,
        )

    def arrived(ref, i):
        pltpu.make_async_copy(ref, ref, recv_sem.at[i]).wait()

    def departed(ref, i):
        pltpu.make_async_copy(ref, ref, send_sem.at[i]).wait()

    loads[0].wait()
    for c in range(2):
        hid32[c] = hid[:, HD * c : HD * c + HD].astype(F32)
    rows = jnp.concatenate(
        [
            jnp.concatenate(
                [hid32[c, pl.ds(16 * g + t, 8, stride=2), :] for g in range(4) for t in range(2)], axis=0
            )
            for c in range(2)
        ],
        axis=1,
    )
    squares = jnp.sum(rows * rows, axis=1, keepdims=True)
    spread = jnp.where(iota((64, HD), 0) == iota((64, HD), 1), squares, 0.0)
    sq_src[...] = jnp.sum(spread, axis=0, keepdims=True)
    loads[10].wait()
    normed = (rows * gain[...].astype(F32).reshape(1, 256)).astype(BF16)
    loads[1].wait()
    raw = jnp.dot(normed, wq[...], preferred_element_type=F32).astype(BF16)
    for h in range(8):
        for g in range(4):
            q_src[4 * h + g] = raw[16 * g : 16 * g + 16, HD * h : HD * h + HD]
    loads[2].wait()
    loads[3].wait()
    raw = jnp.dot(normed, wkv[...], preferred_element_type=F32).astype(BF16)
    for g in range(4):
        for k in range(2):
            kv_src[g, 16 * k : 16 * k + 16, :] = raw[16 * g : 16 * g + 16, HD * k : HD * k + HD]

    pl.semaphore_wait(barrier, N_INST - 1 + N_TP - 1)

    @pl.when(is_low)
    def _():
        for to in peers:
            remote(q_src.at[to], q_rcv.at[0, inst], 1, {"inst": to, "tp": high}, 0).start()
        remote(q_src.at[inst], q_rcv.at[0, inst], 1, {"inst": inst, "tp": high}, 0).start()

    @pl.when(is_high)
    def _():
        for to in peers:
            remote(q_src.at[to], q_rcv.at[1, inst], 1, {"inst": to, "tp": tp}, 1).start()
            remote(sq_src, sq_rcv.at[inst], 0, {"inst": to, "tp": tp}, 5).start()
        q_rcv[1, inst] = q_src[inst]
        sq_rcv[inst] = sq_src[...]

    for g in range(4):

        @pl.when((inst != g) | is_low)
        def _():
            remote(kv_src.at[g], kv_rcv.at[core, inst], 2, {"inst": g, "tp": high}, 2 + core).start()

    @pl.when(is_low)
    def _():
        remote(wo_hbm, wo.at[0], 9, {"inst": inst, "tp": high}, 7).start()

    loads[6].wait()

    loads[4].wait()
    loads[5].wait()
    row = iota((16, 512), 0)
    shifted = iota((16, 512), 1) - ((row // 2) * 64 + lax.rem(row, 2) * 8)
    column = iota((1, 512), 1)

    def slot(s, targets):
        owner = owns[s]
        safe = jnp.maximum(owner, 0)
        target = jnp.where(owner >= 0, (safe // 8) * 16 + lax.rem(safe, 8), -1000)
        limit = jnp.where(owner >= 0, lens[safe] - pages[s] * 256, 0)
        sel[pl.ds(pl.multiple_of(16 * s, 16), 16), :] = (shifted == target).astype(F32).astype(BF16)
        bias[s] = jnp.where(iota((1, 256), 1) < limit, 0.0, NEG)
        member[s] = (iota((1, HD), 1) == owner).astype(jnp.int32)
        return jnp.where(column // 16 == s, target, targets)

    targets = lax.fori_loop(0, 32, slot, jnp.zeros((1, 512), jnp.int32), unroll=4)
    j = lax.rem(column, 16)
    targets = targets + (j // 2) * 64 + lax.rem(j, 2) * 8
    turned = lax.rem(iota((512, 512), 0) + 64 * lax.rem(z + 2, 8), 512)
    sel_t[...] = (turned == targets).astype(F32).astype(BF16)

    @pl.when(is_high)
    def _():
        loads[9].start()
        spot = iota((16, HD), 0)
        lane = iota((16, HD), 1)
        position = jnp.zeros((16, HD), jnp.int32)
        for k in range(8):
            position = jnp.where(lax.rem(spot, 8) == k, lens[8 * x + k], position)
        position = position + spot // 8
        index = lax.rem(lane, 64).astype(F32)
        angle = position.astype(F32) * jnp.exp(index * (-2.0 / HD * 13.122363377404328))
        cosine = jnp.cos(angle)
        sine = jnp.sin(angle) * jnp.where(lane < 64, -1.0, 1.0)
        arrived(sq_rcv.at[0:31], 5)
        total = jnp.sum(sq_rcv[...], axis=0)
        mine = jnp.where(lane == 16 * x + spot, total, 0.0)
        inverse = lax.rsqrt(jnp.sum(mine, axis=1, keepdims=True) / D + EPS)
        arrived(q_rcv.at[1, 0:31], 1)
        joined = jnp.sum(q_rcv[1].astype(F32), axis=0)
        q_all[inst] = rope(joined * inverse, cosine, sine).astype(BF16)
        for to in peers:
            remote(q_all.at[inst], q_all.at[inst], 10, {"inst": to, "tp": tp}, 4).start()
        arrived(q_rcv.at[0], 0)
        joined = jnp.sum(q_rcv[0].astype(F32), axis=0)
        q_low[...] = rope(joined * inverse, cosine, sine).astype(BF16)
        for to in peers:
            remote(q_low, q_all.at[inst], 3, {"inst": to, "tp": low}, 4).start()
        remote(q_low, q_all.at[inst], 3, {"inst": inst, "tp": low}, 4).start()

        @pl.when(z == 0)
        def _():
            kv_rcv[1, inst] = kv_src[x]
            arrived(kv_rcv.at[0], 2)
            arrived(kv_rcv.at[1, 0:31], 3)
            for c in range(2):
                both = jnp.sum(kv_rcv[c].astype(F32), axis=0)
                both = both * jnp.concatenate([inverse, inverse], axis=0)
                kv_new[c, 0:16, :] = rope(both[0:16], cosine, sine).astype(BF16)
                kv_new[c, 16:32, :] = both[16:32].astype(BF16)
            for k in range(1, 8):
                remote(kv_new, kv_new, 4, {"inst": 4 * k + x, "tp": tp}, 6).start()

    loads[7].wait()
    loads[8].wait()

    @pl.when(is_low)
    def _():
        arrived(q_all, 4)

    @pl.when(is_high)
    def _():
        arrived(q_all.at[0:31], 4)

    queries = jnp.dot(sel[...], q_all[...].reshape(512, HD), preferred_element_type=F32).astype(BF16)
    scores = lax.dot_general(
        queries.reshape(32, 16, HD), keys[...], (((2,), (2,)), ((0,), (0,))), preferred_element_type=F32
    )
    scores = scores * SCALE + bias[...]
    top = jnp.max(scores, axis=2, keepdims=True)
    weights = jnp.exp(scores - top)
    weight_sum = jnp.sum(weights, axis=2, keepdims=True)
    part = lax.dot_general(
        weights.astype(BF16), vals[...], (((2,), (1,)), ((0,), (0,))), preferred_element_type=F32
    )
    belongs = member[...] > 0
    top_req = jnp.max(jnp.where(belongs, top, NEG), axis=0)
    peak = jnp.max(jnp.where(belongs, top_req[None], NEG), axis=2, keepdims=True)
    factor = jnp.exp(top - peak)
    sum_req = jnp.sum(jnp.where(belongs, factor * weight_sum, 0.0), axis=0)
    stats = jnp.where(iota((16, HD), 1) < 32, top_req, pltpu.roll(sum_req, 32, 1))
    st_src[...] = stats.reshape(8, 2, HD)
    part = (part * factor).reshape(512, HD)
    high_part = part.astype(BF16)
    low_part = (part - high_part.astype(F32)).astype(BF16)
    parts = jnp.concatenate([high_part, low_part], axis=1)

    def send_part(dz, dx):
        zo, xo = lax.rem(z + dz, 8), lax.rem(x + dx, 4)
        to = {"inst": zo * 4 + xo, "tp": high}
        held = acc_src.at[4 * ((dz - 2) % 8) + xo]
        remote(held, acc_rcv.at[core, inst], 6, to, 10 + core).start()
        remote(st_src.at[zo], st_rcv.at[core, inst], 5, to, 8 + core).start()

    for half in range(2):
        rows = slice(256 * half, 256 * half + 256)
        both = jnp.dot(sel_t[rows, :], parts, preferred_element_type=F32)
        both = (both[:, :HD] + both[:, HD:]).astype(BF16)
        acc_src[16 * half : 16 * half + 16] = both.reshape(16, 16, HD)
        for dz, dx in offsets:
            if ((dz - 2) % 8 >= 4) == half:
                send_part(dz, dx)

    @pl.when(is_low)
    def _():
        send_part(0, 0)

    @pl.when(is_high)
    def _():
        acc_rcv[1, inst] = acc_src[24 + x]
        st_rcv[1, inst] = st_src[z]

        @pl.when(z > 0)
        def _():
            arrived(kv_new, 6)

        row = iota((16, 16), 0)
        key = iota((16, 16), 1)
        seen = (lax.rem(row, 8) == lax.rem(key, 8)) & (key // 8 <= row // 8)
        fresh_tops, fresh_sums, fresh_outs = [], [], []
        for c in range(2):
            query = q_all[inst] if c else q_low[...]
            fresh = lax.dot_general(
                query, kv_new[c, 0:16, :], (((1,), (1,)), ((), ())), preferred_element_type=F32
            ) * SCALE
            fresh = jnp.where(seen, fresh, NEG)
            fresh_top = jnp.max(fresh, axis=1, keepdims=True)
            weights = jnp.where(seen, jnp.exp(fresh - fresh_top), 0.0)
            fresh_tops.append(fresh_top)
            fresh_sums.append(jnp.sum(weights, axis=1, keepdims=True))
            fresh_outs.append(
                jnp.dot(weights.astype(BF16), kv_new[c, 16:32, :], preferred_element_type=F32)
            )

        for c in (1, 0):
            arrived(st_rcv.at[1, 0:31] if c else st_rcv.at[0], 8 + c)
            stats = jnp.concatenate([st_rcv[c, :, 0, :], st_rcv[c, :, 1, :]], axis=0)
            stats = pltpu.roll(stats, lax.rem(HD - 8 * x, HD), 1).T
            tops, sums = stats[0:8], stats[32:40]
            scales, fresh_scales, totals = [], [], []
            for t in range(2):
                first = fresh_tops[c][8 * t : 8 * t + 8]
                held = tops[:, 32 * t : 32 * t + 32]
                peak = jnp.maximum(jnp.max(held, axis=1, keepdims=True), first)
                scale = jnp.exp(held - peak)
                fresh_scale = jnp.exp(first - peak)
                total = jnp.sum(scale * sums[:, 32 * t : 32 * t + 32], axis=1, keepdims=True)
                totals.append(total + fresh_scale * fresh_sums[c][8 * t : 8 * t + 8])
                scales.append(scale)
                fresh_scales.append(fresh_scale)
            scale = jnp.concatenate(scales, axis=0)
            arrived(acc_rcv.at[1, 0:31] if c else acc_rcv.at[0], 10 + c)
            out = jnp.concatenate(fresh_scales, axis=0) * fresh_outs[c]
            for d in range(N_INST):
                out = out + scale[:, d : d + 1] * acc_rcv[c, d].astype(F32)
            att_all[x, z, c] = (out / jnp.concatenate(totals, axis=0)).astype(BF16)

        for k in range(N_INST - 1):
            to = k + (k >= inst).astype(jnp.int32)
            group = lax.rem(x - lax.rem(to, 4) + 4, 4)
            remote(att_all.at[x, z], att_all.at[x, z], 7, {"inst": to, "tp": tp}, 12 + group).start()

        loads[9].wait()
        arrived(wo.at[0], 7)
        for k in (0, 1, 3, 2):
            g = lax.rem(x + k, 4)
            arrived(att_all.at[g] if k else att_all.at[g, 0:7], 12 + k)
            attention = jnp.concatenate([att_all[g, h, c] for c in range(2) for h in range(8)], axis=1)
            projected = jnp.dot(attention, wo[...].reshape(2048, 256), preferred_element_type=F32)
            tp_all[y, g] = projected.astype(BF16)
            for to in tp_peers:
                remote(tp_all.at[y, g], tp_all.at[y, g], 8, {"inst": inst, "tp": to}, 16 + k).start()

    for k in (0, 1, 3, 2):
        g = lax.rem(x + k, 4)

        @pl.when(is_low)
        def _():
            arrived(tp_all.at[:, g], 16 + k)

        @pl.when(is_high)
        def _():
            arrived(tp_all.at[0:3, g], 16 + k)

        mixed = tp_all[0, g].astype(F32)
        for d in range(1, 4):
            mixed = mixed + tp_all[d, g].astype(F32)
        for t in range(2):
            for c in range(2):
                held = mixed[8 * t : 8 * t + 8, HD * c : HD * c + HD]
                out_ref[c, g, pl.ds(t, 8, stride=2), :] = held

    @pl.when(is_low)
    def _():
        departed(q_rcv.at[0], 1)
        departed(kv_src, 2)
        departed(st_rcv.at[0], 5)
        departed(acc_rcv.at[0], 6)
        departed(wo.at[0], 9)

    @pl.when(is_high)
    def _():
        departed(sq_rcv.at[0:31], 0)
        departed(q_rcv.at[1, 0:31], 1)

        @pl.when(z == 0)
        def _():
            departed(kv_src.at[0:3], 2)
            departed(kv_rcv.at[0, 0:14], 4)

        @pl.when(z > 0)
        def _():
            departed(kv_src, 2)

        departed(q_rcv.at[0], 3)
        departed(q_rcv.at[1, 0:31], 10)
        departed(st_rcv.at[1, 0:31], 5)
        departed(acc_rcv.at[1, 0:31], 6)
        departed(acc_rcv.at[:, 0:31], 7)
        departed(wo.at[0, 0:448], 8)


def on_device(*arrays):
    hbm = pl.BlockSpec(memory_space=pltpu.HBM)
    vmem = pl.BlockSpec(memory_space=pltpu.VMEM)
    mixed = pl.pallas_call(
        kernel,
        out_shape=pltpu.VMEM((2, 4, 16, HD), F32),
        in_specs=[hbm] * 10,
        out_specs=vmem,
        scratch_shapes=[
            pltpu.VMEM((64, 256), BF16),
            pltpu.VMEM((2, 64, HD), F32),
            pltpu.VMEM((256,), BF16),
            pltpu.VMEM((256, 1024), BF16),
            pltpu.VMEM((256, 256), BF16),
            pltpu.VMEM((2, 1024, 256), BF16),
            pltpu.VMEM((32, 256, HD), BF16),
            pltpu.VMEM((32, 256, HD), BF16),
            pltpu.SMEM((32,), jnp.int32),
            pltpu.SMEM((32,), jnp.int32),
            pltpu.SMEM((32,), jnp.int32),
            pltpu.VMEM((N_INST, 16, HD), BF16),
            pltpu.VMEM((2, N_INST, 16, HD), BF16),
            pltpu.VMEM((4, 32, HD), BF16),
            pltpu.VMEM((2, N_INST, 32, HD), BF16),
            pltpu.VMEM((1, HD), F32),
            pltpu.VMEM((N_INST, 1, HD), F32),
            pltpu.VMEM((N_INST, 16, HD), BF16),
            pltpu.VMEM((16, HD), BF16),
            pltpu.VMEM((2, 32, HD), BF16),
            pltpu.VMEM((512, 512), BF16),
            pltpu.VMEM((512, 512), BF16),
            pltpu.VMEM((32, 1, 256), F32),
            pltpu.VMEM((32, 1, HD), jnp.int32),
            pltpu.VMEM((N_INST, 16, HD), BF16),
            pltpu.VMEM((2, N_INST, 16, HD), BF16),
            pltpu.VMEM((8, 2, HD), F32),
            pltpu.VMEM((2, N_INST, 2, HD), F32),
            pltpu.VMEM((4, 8, 2, 16, HD), BF16),
            pltpu.VMEM((4, 4, 16, 256), BF16),
            pltpu.SemaphoreType.DMA((11,)),
            pltpu.SemaphoreType.DMA((11,)),
            pltpu.SemaphoreType.DMA((20,)),
        ],
        compiler_params=pltpu.CompilerParams(
            collective_id=0, has_side_effects=True, vmem_limit_bytes=48 * 1024 * 1024
        ),
        name="paged_attention",
    )(*(pltpu.with_memory_space_constraint(a, pltpu.HBM) for a in arrays))
    return mixed.transpose(1, 2, 0, 3).reshape(64, 256).astype(BF16)


def solution(mesh):
    return jax.shard_map(
        on_device,
        mesh=mesh,
        in_specs=(
            P(None, "inst"),
            P("inst"),
            P("inst", "tp"),
            P("inst", "tp"),
            P("inst", "tp"),
            P("tp", "inst"),
            P(None, "inst", None, "tp"),
            P(),
            P("inst"),
            P("inst"),
        ),
        out_specs=P(None, "inst"),
        check_vma=False,
    )
```

time: 44.5 us -> 41.2 us (0.926)
  Pallas kernels: 43.7 us -> 40.4 us
    pallas_call x1, Pallas kernels: 43.7 us -> 40.4 us  [on_device(): pl.pallas_call(kernel, out_shape=pltpu.VMEM((2, 4, 16, HD), F32), in_spec...]
where the time goes in v4:
time: 41.2 us; the launch traced here: 41.1 us
  Pallas kernels  40.4 us (98%)
  local copies, waits for them, and re-layouts  0.66 us (2%)
    pallas_call x1, Pallas kernels, on_device(): pl.pallas_call(kernel, out_shape=pltpu.VMEM((2, 4, 16, HD), F32), in_spec...  40.4 us

profile of v4, /device:TPU:1, one launch (start us, length us, event | category | flops | bytes accessed | tf_op | source)
XLA Modules:
  0.0 41.1 jit_solution(11755650038998015752)
XLA Ops:
  0.0 40.4 %paged_attention.1 = f32[2,4,16,128]{3,2,1,0:T(8,128)S(1)} custom-call(bf16[64,256]{1,0:T(8,128)(2,1)} %hid_hbm.1, bf16[256]{0:T(256)(128)(2,1)} %gain_hbm.1, bf16[256,1024]{1,0:T(8,128)(2,1)} %wq_hbm.1, bf16[256,128]{1,0:T(8,128)(2,1)} %wk_hbm.1, bf16[256,128]{1,0:T(8,128)(2,1)} %wv_hbm.1, bf16[1024,256]{1,0:T(8,128)(2,1)} %wo_hbm.1, ...), custom_call_target="tpu_custom_call" | custom-call | tf_op jit(solution)/shard_map/paged_attention/pallas_call | solution.py:392
  40.5 0.6 %copy.14 = bf16[8,8,2,128]{3,1,2,0:T(8,128)(2,1)} copy(bf16[8,8,2,128]{3,2,1,0:T(2,128)(2,1)S(1)} %bitcast.7) | data formatting | bytes 65536
  (2 shorter events, 0.0 us)

commit v5 on v4

--- a/solution.py
+++ b/solution.py
@@ -246,6 +246,13 @@
     sum_req = jnp.sum(jnp.where(belongs, factor * weight_sum, 0.0), axis=0)
     stats = jnp.where(iota((16, HD), 1) < 32, top_req, pltpu.roll(sum_req, 32, 1))
     st_src[...] = stats.reshape(8, 2, HD)
+    def send_stats(dz, dx):
+        zo, xo = lax.rem(z + dz, 8), lax.rem(x + dx, 4)
+        to = {"inst": zo * 4 + xo, "tp": high}
+        remote(st_src.at[zo], st_rcv.at[core, inst], 5, to, 8 + core).start()
+
+    for dz, dx in offsets[:31]:
+        send_stats(dz, dx)
     part = (part * factor).reshape(512, HD)
     high_part = part.astype(BF16)
     low_part = (part - high_part.astype(F32)).astype(BF16)
@@ -256,7 +263,6 @@
         to = {"inst": zo * 4 + xo, "tp": high}
         held = acc_src.at[4 * ((dz - 2) % 8) + xo]
         remote(held, acc_rcv.at[core, inst], 6, to, 10 + core).start()
-        remote(st_src.at[zo], st_rcv.at[core, inst], 5, to, 8 + core).start()
 
     for half in range(2):
         rows = slice(256 * half, 256 * half + 256)
@@ -270,6 +276,7 @@
     @pl.when(is_low)
     def _():
         send_part(0, 0)
+        send_stats(0, 0)
 
     @pl.when(is_high)
     def _():

time: 41.2 us -> 41 us (level)
  no operation moved by 1% of the time
where the time goes in v5:
time: 41 us; the launch traced here: 40.9 us
  Pallas kernels  40.2 us (98%)
  local copies, waits for them, and re-layouts  0.66 us (2%)
    pallas_call x1, Pallas kernels, on_device(): pl.pallas_call(kernel, out_shape=pltpu.VMEM((2, 4, 16, HD), F32), in_spec...  40.2 us

profile of v5, /device:TPU:1, one launch (start us, length us, event | category | flops | bytes accessed | tf_op | source)
XLA Modules:
  0.0 40.9 jit_solution(11115122996259021929)
XLA Ops:
  0.0 40.2 %paged_attention.1 = f32[2,4,16,128]{3,2,1,0:T(8,128)S(1)} custom-call(bf16[64,256]{1,0:T(8,128)(2,1)} %hid_hbm.1, bf16[256]{0:T(256)(128)(2,1)} %gain_hbm.1, bf16[256,1024]{1,0:T(8,128)(2,1)} %wq_hbm.1, bf16[256,128]{1,0:T(8,128)(2,1)} %wk_hbm.1, bf16[256,128]{1,0:T(8,128)(2,1)} %wv_hbm.1, bf16[1024,256]{1,0:T(8,128)(2,1)} %wo_hbm.1, ...), custom_call_target="tpu_custom_call" | custom-call | tf_op jit(solution)/shard_map/paged_attention/pallas_call | solution.py:399
  40.3 0.6 %copy.14 = bf16[8,8,2,128]{3,1,2,0:T(8,128)(2,1)} copy(bf16[8,8,2,128]{3,2,1,0:T(2,128)(2,1)S(1)} %bitcast.7) | data formatting | bytes 65536
  (2 shorter events, 0.0 us)

commit v6 on v5

--- a/solution.py
+++ b/solution.py
@@ -254,9 +254,7 @@
     for dz, dx in offsets[:31]:
         send_stats(dz, dx)
     part = (part * factor).reshape(512, HD)
-    high_part = part.astype(BF16)
-    low_part = (part - high_part.astype(F32)).astype(BF16)
-    parts = jnp.concatenate([high_part, low_part], axis=1)
+    parts = part.astype(BF16)
 
     def send_part(dz, dx):
         zo, xo = lax.rem(z + dz, 8), lax.rem(x + dx, 4)
@@ -267,7 +265,7 @@
     for half in range(2):
         rows = slice(256 * half, 256 * half + 256)
         both = jnp.dot(sel_t[rows, :], parts, preferred_element_type=F32)
-        both = (both[:, :HD] + both[:, HD:]).astype(BF16)
+        both = both.astype(BF16)
         acc_src[16 * half : 16 * half + 16] = both.reshape(16, 16, HD)
         for dz, dx in offsets:
             if ((dz - 2) % 8 >= 4) == half:

time: 41 us -> 40.9 us (level)
  no operation moved by 1% of the time
where the time goes in v6:
time: 40.9 us; the launch traced here: 40.8 us
  Pallas kernels  40.2 us (98%)
  local copies, waits for them, and re-layouts  0.66 us (2%)
    pallas_call x1, Pallas kernels, on_device(): pl.pallas_call(kernel, out_shape=pltpu.VMEM((2, 4, 16, HD), F32), in_spec...  40.2 us

profile of v6, /device:TPU:1, one launch (start us, length us, event | category | flops | bytes accessed | tf_op | source)
XLA Modules:
  0.0 40.8 jit_solution(10768856592649921537)
XLA Ops:
  0.0 40.2 %paged_attention.1 = f32[2,4,16,128]{3,2,1,0:T(8,128)S(1)} custom-call(bf16[64,256]{1,0:T(8,128)(2,1)} %hid_hbm.1, bf16[256]{0:T(256)(128)(2,1)} %gain_hbm.1, bf16[256,1024]{1,0:T(8,128)(2,1)} %wq_hbm.1, bf16[256,128]{1,0:T(8,128)(2,1)} %wk_hbm.1, bf16[256,128]{1,0:T(8,128)(2,1)} %wv_hbm.1, bf16[1024,256]{1,0:T(8,128)(2,1)} %wo_hbm.1, ...), custom_call_target="tpu_custom_call" | custom-call | tf_op jit(solution)/shard_map/paged_attention/pallas_call | solution.py:397
  40.2 0.6 %copy.14 = bf16[8,8,2,128]{3,1,2,0:T(8,128)(2,1)} copy(bf16[8,8,2,128]{3,2,1,0:T(2,128)(2,1)S(1)} %bitcast.7) | data formatting | bytes 65536
  (2 shorter events, 0.0 us)
